TPU v7x, 32 devices: a whole 2x2x4 slice. The times are simulated.
32 devices in a mesh: groups: 2 (over y), row: 4 (over z), col: 4 (over x, core).
Axes of the slice: x: 2, y: 2, z: 4, core: 2. Of those that a mesh axis runs over, the one named last changes fastest.
Arguments:
- grad_x: bfloat16 [3, 3072, 1536], P(None, ('groups', 'row'), 'col'), parts along dimension 1, may hold values from -4 to 4
- grad_y: bfloat16 [3, 3072, 1536], P(None, ('groups', 'row'), 'col'), parts along dimension 1, may hold values from -4 to 4
- seam_mask: int32 [3072, 1536], P(('groups', 'row'), 'col'), parts along dimension 0, may hold values 0 or 1
- tile_offset: int32 [3, 8, 4], P(None, 'groups'), parts along dimension 1, may hold values from -8 to 8
Outputs:
- stitched: float32 [3, 3072, 1536], P(None, ('groups', 'row'), 'col'), parts along dimension 1
There are 2 independent parts, one for each index of `groups`. A program takes and returns all parts, laid end to end along the dimension named above; each array names one. Nothing has to cross between parts.
Inputs may be any that keep to these rules, and one draw needn't show every extreme that they name: `tile_offset`: whole quarter steps of exposure.
All inputs are finite; a program needn't handle non-finite values. No bound on the sum of `seam_mask` on one device may be relied on, other than what follows from the above.
Results may differ from a plain program's by a relative error of at most 0.0045.
Values sent between devices are 32-bit elements; how exact they have to be, the bound alone decides.
A program may use at most 64 MiB of HBM per device.

v0:
```python
import math

import jax
import jax.numpy as jnp
from jax import lax
from jax.sharding import PartitionSpec as P

M = 128
SWEEPS = 8


def shifted(x, axis, by):
    length = lax.axis_size(axis)
    pairs = [(i, i + by) for i in range(length) if 0 <= i + by < length]
    return lax.ppermute(x, axis, pairs)


def with_halo(x, sides, width):
    for axis, dim in sides:
        size, length = (lax.axis_size(axis), x.shape[dim])
        up = [(i, (i + 1) % size) for i in range(size - 1)]
        down = [(j, i) for i, j in up]
        last = lax.slice_in_dim(x, length - width, length, axis=dim)
        first = lax.slice_in_dim(x, 0, width, axis=dim)
        before = lax.ppermute(last, axis, up)
        after = lax.ppermute(first, axis, down)
        x = jnp.concatenate([before, x, after], axis=dim)
    return x


def cosine_table(count, modes, start, length):
    order = jnp.arange(modes, dtype=jnp.int32)
    places = start + jnp.arange(length, dtype=jnp.int32)
    phases = order[:, None] * (2 * places[None, :] + 1) % (4 * count)
    angles = math.pi / (2 * count) * phases.astype(jnp.float32)
    scales = jnp.where(order == 0, math.sqrt(1.0 / count), math.sqrt(2.0 / count)).astype(
        jnp.float32
    )
    return scales[:, None] * jnp.cos(angles)


def eigen_line(count, length):
    order = jnp.arange(length, dtype=jnp.int32).astype(jnp.float32)
    return 2.0 - 2.0 * jnp.cos(math.pi / count * order)


def neighbour_sum(padded):
    return padded[:, :-2, 1:-1] + padded[:, 2:, 1:-1] + padded[:, 1:-1, :-2] + padded[:, 1:-1, 2:]


def inside_count(places, count):
    return (places > 0).astype(jnp.float32) + (places < count - 1).astype(jnp.float32)


def body(grad_x, grad_y, seam_mask, tile_offset):
    channels, tile_rows, tile_cols = grad_x.shape
    row_count = lax.axis_size("row")
    col_count = lax.axis_size("col")
    total_rows = tile_rows * row_count
    total_cols = tile_cols * col_count
    row_index = lax.axis_index("row")
    col_index = lax.axis_index("col")
    highest = lax.Precision.HIGHEST
    damping = 1.0 - 0.75 * seam_mask.astype(jnp.float32)
    edge_x = grad_x.astype(jnp.float32) * damping
    edge_y = grad_y.astype(jnp.float32) * damping
    levels = 0.25 * tile_offset.astype(jnp.float32)
    anchor = jnp.int32(0)
    below_row = jnp.minimum(row_index + 1, row_count - 1)
    right_col = jnp.minimum(col_index + 1, col_count - 1)
    here = lax.dynamic_slice(levels, (anchor, row_index, col_index), (channels, 1, 1))
    below = lax.dynamic_slice(levels, (anchor, below_row, col_index), (channels, 1, 1))
    right = lax.dynamic_slice(levels, (anchor, row_index, right_col), (channels, 1, 1))
    local_rows = jnp.arange(tile_rows, dtype=jnp.int32)
    local_cols = jnp.arange(tile_cols, dtype=jnp.int32)
    global_rows = row_index * tile_rows + local_rows
    global_cols = col_index * tile_cols + local_cols
    last_row = (local_rows == tile_rows - 1).astype(jnp.float32)[:, None]
    last_col = (local_cols == tile_cols - 1).astype(jnp.float32)[None, :]
    edge_x = (edge_x + last_row * (below - here)) * (global_rows < total_rows - 1).astype(
        jnp.float32
    )[:, None]
    edge_y = (edge_y + last_col * (right - here)) * (global_cols < total_cols - 1).astype(
        jnp.float32
    )[None, :]
    above_edge = shifted(edge_x[:, tile_rows - 1 :, :], "row", 1)
    left_edge = shifted(edge_y[:, :, tile_cols - 1 :], "col", 1)
    before_x = jnp.concatenate([above_edge, edge_x[:, :-1, :]], axis=1)
    before_y = jnp.concatenate([left_edge, edge_y[:, :, :-1]], axis=2)
    source = -(edge_x - before_x + (edge_y - before_y))
    screen = 0.5 * math.pi * math.pi / (total_rows * total_cols)
    table_x = cosine_table(total_rows, M, row_index * tile_rows, tile_rows)
    table_y = cosine_table(total_cols, M, col_index * tile_cols, tile_cols)
    halves = jnp.einsum("cij,lj->cil", source, table_y, precision=highest)
    partial_modes = jnp.einsum("ki,cil->ckl", table_x, halves, precision=highest)
    eigen_cols = eigen_line(total_cols, M)[None, :]
    spectral = lax.psum(partial_modes, ("row", "col"))
    coeffs = spectral / (screen + eigen_line(total_rows, M)[:, None] + eigen_cols)
    backed = jnp.einsum("ckl,lj->ckj", coeffs, table_y, precision=highest)
    stitched = jnp.einsum("ki,ckj->cij", table_x, backed, precision=highest)
    counts = (
        inside_count(global_rows, total_rows)[:, None]
        + inside_count(global_cols, total_cols)[None, :]
    )
    denominator = screen + counts
    for sweep_index in range(SWEEPS):
        padded = with_halo(stitched, (("row", 1), ("col", 2)), 1)
        stitched = (source + neighbour_sum(padded)) / denominator
    return stitched


def solution(mesh):
    in_specs = (
        P(None, ("groups", "row"), "col"),
        P(None, ("groups", "row"), "col"),
        P(("groups", "row"), "col"),
        P(None, "groups", None),
    )
    out_specs = P(None, ("groups", "row"), "col")
    return jax.shard_map(body, mesh=mesh, in_specs=in_specs, out_specs=out_specs, check_vma=False)
```

profile of v0, /device:TPU:0, one launch (start us, length us, event | category | flops | bytes accessed | tf_op | source)
XLA Modules:
  0.0 335.6 jit_solution(8586324488082109092)
XLA Ops:
  14.7 2.9 collective-permute-start.1
  18.2 4.9 %collective-permute-start = (f32[3,1,384]{2,1,0:T(1,128)}, f32[3,1,384]{2,1,0:T(1,128)}, u32[]{:S(2)}, u32[]{:S(2)}) collective-permute-start(f32[3,1,384]{2,1,0:T(1,128)} %slice.304), channel_id=1, source_target_pairs={{0,4},{4,8},{8,12},{1,5},{5,9},{9,13},{2,6},{6,10},{10,14},{3,7},{... | collective-permute-start | bytes 13832 | tf_op jit(solution)/shard_map/ppermute | solution.py:15
  27.2 3.4 %fusion.41 = f32[3,384,384]{2,1,0:T(8,128)S(1)} fusion(f32[3,383,384]{2,1,0:T(8,128)} %bitcast.20, f32[3,1,384]{2,1,0:T(1,128)} %collective-permute-done, f32[3,384,383]{2,1,0:T(8,128)S(1)} %bitcast.19, f32[3,384,1]{2,1,0:T(8,128)} %copy.6, f32[384]{0:T(512)} %copy-done.16, f32[3,384]{1,0:T(4,128)S(1)} %get-tuple-element.41, ...), kind=kLoop, calls=%fused_computation.106 | loop fusion | flops 6193152 | bytes 7680000 | tf_op jit(solution)/shard_map/neg | solution.py:90
  30.7 2.6 fusion.61
  35.6 88.9 %all-reduce.2.cloned.1.call-done = f32[3,128,128]{1,2,0:T(8,128)} async-done(((f32[3,128,128]{1,2,0:T(8,128)}), f32[3,128,128]{1,2,0:T(8,128)}) %all-reduce.2.cloned.1.call-update) | async-done | bytes 196624 | tf_op jit(solution)/shard_map/psum | solution.py:97
  124.5 2.5 fusion.52
  129.3 3.3 collective-permute-start.2
  134.0 4.2 %collective-permute-done.3 = f32[3,1,384]{2,1,0:T(1,128)S(1)} collective-permute-done((f32[3,1,384]{2,1,0:T(1,128)S(1)}, f32[3,1,384]{2,1,0:T(1,128)S(1)}, u32[]{:S(2)}, u32[]{:S(2)}) %collective-permute-start.3) | collective-permute-done | bytes 4640 | tf_op jit(solution)/shard_map/ppermute | solution.py:26
  145.3 4.9 %fusion.37 = f32[3,384,384]{2,1,0:T(8,128)S(1)} fusion(f32[3,384,384]{2,1,0:T(8,128)S(1)} %fusion.41, f32[3,386,1]{2,1,0:T(8,128)} %copy.15, f32[3,1,384]{2,1,0:T(1,128)S(1)} %collective-permute-done.3, f32[3,384,384]{2,1,0:T(8,128)} %copy-done.1, f32[3,1,384]{2,1,0:T(1,128)S(1)} %collective-permute-done.2, f32[3,386,1]{2,1,0:T(8,128)S(1)} %copy.13, ...), kind=kLoop, calls=%fused_computation.94 | loop fusion | flops 5750784 | bytes 5916720 | tf_op jit(solution)/shard_map/div | solution.py:108
  150.2 3.3 collective-permute-start.6
  154.9 4.2 %collective-permute-done.7 = f32[3,1,384]{2,1,0:T(1,128)S(1)} collective-permute-done((f32[3,1,384]{2,1,0:T(1,128)S(1)}, f32[3,1,384]{2,1,0:T(1,128)S(1)}, u32[]{:S(2)}, u32[]{:S(2)}) %collective-permute-start.7) | collective-permute-done | bytes 4640 | tf_op jit(solution)/shard_map/ppermute | solution.py:26
  162.4 3.4 %collective-permute-start.8 = (f32[3,386,1]{1,2,0:T(1,128)}, f32[3,386,1]{1,2,0:T(1,128)}, u32[]{:S(2)}, u32[]{:S(2)}) collective-permute-start(f32[3,386,1]{1,2,0:T(1,128)} %copy.16), channel_id=1, source_target_pairs={{0,1},{1,2},{2,3},{4,5},{5,6},{6,7},{8,9},{9,10},{10,11},{12,13},{... | collective-permute-start | bytes 13904 | tf_op jit(solution)/shard_map/ppermute | solution.py:25
  173.3 3.9 %fusion.32 = f32[3,384,384]{2,1,0:T(8,128)S(1)} fusion(f32[3,384,384]{2,1,0:T(8,128)S(1)} %fusion.41, f32[3,386,1]{2,1,0:T(8,128)} %copy.19, f32[3,1,384]{2,1,0:T(1,128)S(1)} %collective-permute-done.7, f32[3,384,384]{2,1,0:T(8,128)S(1)} %copy-done.3, f32[3,1,384]{2,1,0:T(1,128)S(1)} %collective-permute-done.6, f32[3,386,1]{2,1,0:T(8,128)} %copy.17, ...), kind=kLoop, calls=%fused_computation.81 | loop fusion | flops 5750784 | bytes 5916720 | tf_op jit(solution)/shard_map/div | solution.py:108
  177.3 2.5 collective-permute-start.10
  181.1 4.2 %collective-permute-done.11 = f32[3,1,384]{2,1,0:T(1,128)S(1)} collective-permute-done((f32[3,1,384]{2,1,0:T(1,128)S(1)}, f32[3,1,384]{2,1,0:T(1,128)S(1)}, u32[]{:S(2)}, u32[]{:S(2)}) %collective-permute-start.11) | collective-permute-done | bytes 4640 | tf_op jit(solution)/shard_map/ppermute | solution.py:26
  188.5 3.4 %collective-permute-start.12 = (f32[3,386,1]{1,2,0:T(1,128)}, f32[3,386,1]{1,2,0:T(1,128)}, u32[]{:S(2)}, u32[]{:S(2)}) collective-permute-start(f32[3,386,1]{1,2,0:T(1,128)} %copy.20), channel_id=1, source_target_pairs={{0,1},{1,2},{2,3},{4,5},{5,6},{6,7},{8,9},{9,10},{10,11},{12,13},{... | collective-permute-start | bytes 13904 | tf_op jit(solution)/shard_map/ppermute | solution.py:25
  199.7 3.9 %fusion.27 = f32[3,384,384]{2,1,0:T(8,128)S(1)} fusion(f32[3,384,384]{2,1,0:T(8,128)S(1)} %fusion.41, f32[3,386,1]{2,1,0:T(8,128)} %copy.23, f32[3,1,384]{2,1,0:T(1,128)S(1)} %collective-permute-done.11, f32[3,384,384]{2,1,0:T(8,128)S(1)} %copy-done.5, f32[3,1,384]{2,1,0:T(1,128)S(1)} %collective-permute-done.10, f32[3,386,1]{2,1,0:T(8,128)} %copy.21, ...), kind=kLoop, calls=%fused_computation.68 | loop fusion | flops 5750784 | bytes 5916720 | tf_op jit(solution)/shard_map/div | solution.py:108
  206.8 4.2 %collective-permute-done.15 = f32[3,1,384]{2,1,0:T(1,128)S(1)} collective-permute-done((f32[3,1,384]{2,1,0:T(1,128)S(1)}, f32[3,1,384]{2,1,0:T(1,128)S(1)}, u32[]{:S(2)}, u32[]{:S(2)}) %collective-permute-start.15) | collective-permute-done | bytes 4640 | tf_op jit(solution)/shard_map/ppermute | solution.py:26
  214.3 3.4 %collective-permute-start.16 = (f32[3,386,1]{1,2,0:T(1,128)}, f32[3,386,1]{1,2,0:T(1,128)}, u32[]{:S(2)}, u32[]{:S(2)}) collective-permute-start(f32[3,386,1]{1,2,0:T(1,128)} %copy.24), channel_id=1, source_target_pairs={{0,1},{1,2},{2,3},{4,5},{5,6},{6,7},{8,9},{9,10},{10,11},{12,13},{... | collective-permute-start | bytes 13904 | tf_op jit(solution)/shard_map/ppermute | solution.py:25
  225.4 3.9 %fusion.22 = f32[3,384,384]{2,1,0:T(8,128)S(1)} fusion(f32[3,384,384]{2,1,0:T(8,128)S(1)} %fusion.41, f32[3,386,1]{2,1,0:T(8,128)} %copy.27, f32[3,1,384]{2,1,0:T(1,128)S(1)} %collective-permute-done.15, f32[3,384,384]{2,1,0:T(8,128)S(1)} %copy-done.7, f32[3,1,384]{2,1,0:T(1,128)S(1)} %collective-permute-done.14, f32[3,386,1]{2,1,0:T(8,128)} %copy.25, ...), kind=kLoop, calls=%fused_computation.55 | loop fusion | flops 5750784 | bytes 5916720 | tf_op jit(solution)/shard_map/div | solution.py:108
  232.6 4.2 %collective-permute-done.19 = f32[3,1,384]{2,1,0:T(1,128)S(1)} collective-permute-done((f32[3,1,384]{2,1,0:T(1,128)S(1)}, f32[3,1,384]{2,1,0:T(1,128)S(1)}, u32[]{:S(2)}, u32[]{:S(2)}) %collective-permute-start.19) | collective-permute-done | bytes 4640 | tf_op jit(solution)/shard_map/ppermute | solution.py:26
  240.1 3.4 %collective-permute-start.20 = (f32[3,386,1]{1,2,0:T(1,128)}, f32[3,386,1]{1,2,0:T(1,128)}, u32[]{:S(2)}, u32[]{:S(2)}) collective-permute-start(f32[3,386,1]{1,2,0:T(1,128)} %copy.28), channel_id=1, source_target_pairs={{0,1},{1,2},{2,3},{4,5},{5,6},{6,7},{8,9},{9,10},{10,11},{12,13},{... | collective-permute-start | bytes 13904 | tf_op jit(solution)/shard_map/ppermute | solution.py:25
  251.2 3.9 %fusion.17 = f32[3,384,384]{2,1,0:T(8,128)S(1)} fusion(f32[3,384,384]{2,1,0:T(8,128)S(1)} %fusion.41, f32[3,386,1]{2,1,0:T(8,128)} %copy.31, f32[3,1,384]{2,1,0:T(1,128)S(1)} %collective-permute-done.19, f32[3,384,384]{2,1,0:T(8,128)S(1)} %copy-done.9, f32[3,1,384]{2,1,0:T(1,128)S(1)} %collective-permute-done.18, f32[3,386,1]{2,1,0:T(8,128)} %copy.29, ...), kind=kLoop, calls=%fused_computation.42 | loop fusion | flops 5750784 | bytes 5916720 | tf_op jit(solution)/shard_map/div | solution.py:108
  258.6 4.0 %collective-permute-done.23 = f32[3,1,384]{2,1,0:T(1,128)S(1)} collective-permute-done((f32[3,1,384]{2,1,0:T(1,128)S(1)}, f32[3,1,384]{2,1,0:T(1,128)S(1)}, u32[]{:S(2)}, u32[]{:S(2)}) %collective-permute-start.23) | collective-permute-done | bytes 4640 | tf_op jit(solution)/shard_map/ppermute | solution.py:26
  265.8 3.4 %collective-permute-start.24 = (f32[3,386,1]{1,2,0:T(1,128)}, f32[3,386,1]{1,2,0:T(1,128)}, u32[]{:S(2)}, u32[]{:S(2)}) collective-permute-start(f32[3,386,1]{1,2,0:T(1,128)} %copy.32), channel_id=1, source_target_pairs={{0,1},{1,2},{2,3},{4,5},{5,6},{6,7},{8,9},{9,10},{10,11},{12,13},{... | collective-permute-start | bytes 13904 | tf_op jit(solution)/shard_map/ppermute | solution.py:25
  277.0 3.9 %fusion.12 = f32[3,384,384]{2,1,0:T(8,128)S(1)} fusion(f32[3,384,384]{2,1,0:T(8,128)S(1)} %fusion.41, f32[3,386,1]{2,1,0:T(8,128)} %copy.35, f32[3,1,384]{2,1,0:T(1,128)S(1)} %collective-permute-done.23, f32[3,384,384]{2,1,0:T(8,128)S(1)} %copy-done.11, f32[3,1,384]{2,1,0:T(1,128)S(1)} %collective-permute-done.22, f32[3,386,1]{2,1,0:T(8,128)} %copy.33, ...), kind=kLoop, calls=%fused_computation.29 | loop fusion | flops 5750784 | bytes 5916720 | tf_op jit(solution)/shard_map/div | solution.py:108
  284.1 4.2 %collective-permute-done.27 = f32[3,1,384]{2,1,0:T(1,128)S(1)} collective-permute-done((f32[3,1,384]{2,1,0:T(1,128)S(1)}, f32[3,1,384]{2,1,0:T(1,128)S(1)}, u32[]{:S(2)}, u32[]{:S(2)}) %collective-permute-start.27) | collective-permute-done | bytes 4640 | tf_op jit(solution)/shard_map/ppermute | solution.py:26
  288.8 2.8 collective-permute-start.28
  297.3 5.2 %fusion.7 = f32[3,384,384]{2,1,0:T(8,128)S(1)} fusion(f32[3,384,384]{2,1,0:T(8,128)S(1)} %fusion.41, f32[3,386,1]{2,1,0:T(8,128)} %copy.39, f32[3,1,384]{2,1,0:T(1,128)S(1)} %collective-permute-done.27, f32[3,384,384]{2,1,0:T(8,128)} %copy-done.12, f32[3,1,384]{2,1,0:T(1,128)S(1)} %collective-permute-done.26, f32[3,386,1]{2,1,0:T(8,128)} %copy.37, ...), kind=kLoop, calls=%fused_computation.16 | loop fusion | flops 5750784 | bytes 5916720 | tf_op jit(solution)/shard_map/div | solution.py:108
  305.8 4.2 %collective-permute-done.31 = f32[3,1,384]{2,1,0:T(1,128)S(1)} collective-permute-done((f32[3,1,384]{2,1,0:T(1,128)S(1)}, f32[3,1,384]{2,1,0:T(1,128)S(1)}, u32[]{:S(2)}, u32[]{:S(2)}) %collective-permute-start.31) | collective-permute-done | bytes 4640 | tf_op jit(solution)/shard_map/ppermute | solution.py:26
  313.1 3.4 %collective-permute-start.32 = (f32[3,386,1]{1,2,0:T(1,128)}, f32[3,386,1]{1,2,0:T(1,128)}, u32[]{:S(2)}, u32[]{:S(2)}) collective-permute-start(f32[3,386,1]{1,2,0:T(1,128)} %copy.40), channel_id=1, source_target_pairs={{0,1},{1,2},{2,3},{4,5},{5,6},{6,7},{8,9},{9,10},{10,11},{12,13},{... | collective-permute-start | bytes 13904 | tf_op jit(solution)/shard_map/ppermute | solution.py:25
  324.0 4.7 %fusion.2 = f32[3,384,384]{2,1,0:T(8,128)} fusion(f32[3,384,384]{2,1,0:T(8,128)S(1)} %fusion.41, f32[3,386,1]{2,1,0:T(8,128)} %copy.43, f32[3,1,384]{2,1,0:T(1,128)S(1)} %collective-permute-done.31, f32[3,384,384]{2,1,0:T(8,128)S(1)} %fusion.7, f32[3,1,384]{2,1,0:T(1,128)S(1)} %collective-permute-done.30, f32[3,386,1]{2,1,0:T(8,128)} %copy.41, ...), kind=kLoop, calls=%fused_computation.3 | loop fusion | flops 5750784 | bytes 5916720 | tf_op jit(solution)/shard_map/div | solution.py:108
  (164 shorter events, 116.3 us)
Async XLA Ops:
  6.5 117.9 %all-reduce.2.cloned.1.call-start = ((), (), s32[]{:S(2)}) async-start(), calls=%async_computation | async-start | bytes 393216 | tf_op jit(solution)/shard_map/psum | solution.py:97
  14.7 10.7 %collective-permute-start.1 = (f32[3,384,1]{1,2,0:T(1,128)}, f32[3,384,1]{1,2,0:T(1,128)}, u32[]{:S(2)}, u32[]{:S(2)}) collective-permute-start(f32[3,384,1]{1,2,0:T(1,128)} %copy.5), channel_id=1, source_target_pairs={{0,1},{1,2},{2,3},{4,5},{5,6},{6,7},{8,9},{9,10},{10,11},{12,13},{... | collective-permute-start | bytes 13832 | tf_op jit(solution)/shard_map/ppermute | solution.py:15
  18.2 9.0 %collective-permute-start = (f32[3,1,384]{2,1,0:T(1,128)}, f32[3,1,384]{2,1,0:T(1,128)}, u32[]{:S(2)}, u32[]{:S(2)}) collective-permute-start(f32[3,1,384]{2,1,0:T(1,128)} %slice.304), channel_id=1, source_target_pairs={{0,4},{4,8},{8,12},{1,5},{5,9},{9,13},{2,6},{6,10},{10,14},{3,7},{... | collective-permute-start | bytes 13832 | tf_op jit(solution)/shard_map/ppermute | solution.py:15
  129.3 4.6 %collective-permute-start.2 = (f32[3,1,384]{2,1,0:T(1,128)S(1)}, f32[3,1,384]{2,1,0:T(1,128)S(1)}, u32[]{:S(2)}, u32[]{:S(2)}) collective-permute-start(f32[3,1,384]{2,1,0:T(1,128)S(1)} %get-tuple-element.37), channel_id=1, source_target_pairs={{0,4},{4,8},{8,12},{1,5},{5,9},{9,13},{2,6},{6,10},{10,14},{3,7},{... | collective-permute-start | bytes 13832 | tf_op jit(solution)/shard_map/ppermute | solution.py:25
  132.6 5.5 %collective-permute-start.3 = (f32[3,1,384]{2,1,0:T(1,128)S(1)}, f32[3,1,384]{2,1,0:T(1,128)S(1)}, u32[]{:S(2)}, u32[]{:S(2)}) collective-permute-start(f32[3,1,384]{2,1,0:T(1,128)S(1)} %get-tuple-element.38), channel_id=1, source_target_pairs={{4,0},{8,4},{12,8},{5,1},{9,5},{13,9},{6,2},{10,6},{14,10},{7,3},{... | collective-permute-start | bytes 13832 | tf_op jit(solution)/shard_map/ppermute | solution.py:26
  140.2 3.9 %collective-permute-start.5 = (f32[3,386,1]{1,2,0:T(1,128)S(1)}, f32[3,386,1]{1,2,0:T(1,128)S(1)}, u32[]{:S(2)}, u32[]{:S(2)}) collective-permute-start(f32[3,386,1]{1,2,0:T(1,128)S(1)} %copy.14), channel_id=1, source_target_pairs={{1,0},{2,1},{3,2},{5,4},{6,5},{7,6},{9,8},{10,9},{11,10},{13,12},{... | collective-permute-start | bytes 13904 | tf_op jit(solution)/shard_map/ppermute | solution.py:26
  150.2 4.7 %collective-permute-start.6 = (f32[3,1,384]{2,1,0:T(1,128)S(1)}, f32[3,1,384]{2,1,0:T(1,128)S(1)}, u32[]{:S(2)}, u32[]{:S(2)}) collective-permute-start(f32[3,1,384]{2,1,0:T(1,128)S(1)} %get-tuple-element.35), channel_id=1, source_target_pairs={{0,4},{4,8},{8,12},{1,5},{5,9},{9,13},{2,6},{6,10},{10,14},{3,7},{... | collective-permute-start | bytes 13832 | tf_op jit(solution)/shard_map/ppermute | solution.py:25
  153.6 5.5 %collective-permute-start.7 = (f32[3,1,384]{2,1,0:T(1,128)S(1)}, f32[3,1,384]{2,1,0:T(1,128)S(1)}, u32[]{:S(2)}, u32[]{:S(2)}) collective-permute-start(f32[3,1,384]{2,1,0:T(1,128)S(1)} %get-tuple-element.36), channel_id=1, source_target_pairs={{4,0},{8,4},{12,8},{5,1},{9,5},{13,9},{6,2},{10,6},{14,10},{7,3},{... | collective-permute-start | bytes 13832 | tf_op jit(solution)/shard_map/ppermute | solution.py:26
  162.4 6.7 %collective-permute-start.8 = (f32[3,386,1]{1,2,0:T(1,128)}, f32[3,386,1]{1,2,0:T(1,128)}, u32[]{:S(2)}, u32[]{:S(2)}) collective-permute-start(f32[3,386,1]{1,2,0:T(1,128)} %copy.16), channel_id=1, source_target_pairs={{0,1},{1,2},{2,3},{4,5},{5,6},{6,7},{8,9},{9,10},{10,11},{12,13},{... | collective-permute-start | bytes 13904 | tf_op jit(solution)/shard_map/ppermute | solution.py:25
  167.8 3.8 %collective-permute-start.9 = (f32[3,386,1]{1,2,0:T(1,128)}, f32[3,386,1]{1,2,0:T(1,128)}, u32[]{:S(2)}, u32[]{:S(2)}) collective-permute-start(f32[3,386,1]{1,2,0:T(1,128)} %copy.18), channel_id=1, source_target_pairs={{1,0},{2,1},{3,2},{5,4},{6,5},{7,6},{9,8},{10,9},{11,10},{13,12},{... | collective-permute-start | bytes 13904 | tf_op jit(solution)/shard_map/ppermute | solution.py:26
  177.3 3.8 %collective-permute-start.10 = (f32[3,1,384]{2,1,0:T(1,128)S(1)}, f32[3,1,384]{2,1,0:T(1,128)S(1)}, u32[]{:S(2)}, u32[]{:S(2)}) collective-permute-start(f32[3,1,384]{2,1,0:T(1,128)S(1)} %get-tuple-element.33), channel_id=1, source_target_pairs={{0,4},{4,8},{8,12},{1,5},{5,9},{9,13},{2,6},{6,10},{10,14},{3,7},{... | collective-permute-start | bytes 13832 | tf_op jit(solution)/shard_map/ppermute | solution.py:25
  179.7 5.5 %collective-permute-start.11 = (f32[3,1,384]{2,1,0:T(1,128)S(1)}, f32[3,1,384]{2,1,0:T(1,128)S(1)}, u32[]{:S(2)}, u32[]{:S(2)}) collective-permute-start(f32[3,1,384]{2,1,0:T(1,128)S(1)} %get-tuple-element.34), channel_id=1, source_target_pairs={{4,0},{8,4},{12,8},{5,1},{9,5},{13,9},{6,2},{10,6},{14,10},{7,3},{... | collective-permute-start | bytes 13832 | tf_op jit(solution)/shard_map/ppermute | solution.py:26
  188.5 6.6 %collective-permute-start.12 = (f32[3,386,1]{1,2,0:T(1,128)}, f32[3,386,1]{1,2,0:T(1,128)}, u32[]{:S(2)}, u32[]{:S(2)}) collective-permute-start(f32[3,386,1]{1,2,0:T(1,128)} %copy.20), channel_id=1, source_target_pairs={{0,1},{1,2},{2,3},{4,5},{5,6},{6,7},{8,9},{9,10},{10,11},{12,13},{... | collective-permute-start | bytes 13904 | tf_op jit(solution)/shard_map/ppermute | solution.py:25
  193.9 4.0 %collective-permute-start.13 = (f32[3,386,1]{1,2,0:T(1,128)}, f32[3,386,1]{1,2,0:T(1,128)}, u32[]{:S(2)}, u32[]{:S(2)}) collective-permute-start(f32[3,386,1]{1,2,0:T(1,128)} %copy.22), channel_id=1, source_target_pairs={{1,0},{2,1},{3,2},{5,4},{6,5},{7,6},{9,8},{10,9},{11,10},{13,12},{... | collective-permute-start | bytes 13904 | tf_op jit(solution)/shard_map/ppermute | solution.py:26
  203.6 3.2 collective-permute-start.14
  205.5 5.5 %collective-permute-start.15 = (f32[3,1,384]{2,1,0:T(1,128)S(1)}, f32[3,1,384]{2,1,0:T(1,128)S(1)}, u32[]{:S(2)}, u32[]{:S(2)}) collective-permute-start(f32[3,1,384]{2,1,0:T(1,128)S(1)} %get-tuple-element.32), channel_id=1, source_target_pairs={{4,0},{8,4},{12,8},{5,1},{9,5},{13,9},{6,2},{10,6},{14,10},{7,3},{... | collective-permute-start | bytes 13832 | tf_op jit(solution)/shard_map/ppermute | solution.py:26
  214.3 6.6 %collective-permute-start.16 = (f32[3,386,1]{1,2,0:T(1,128)}, f32[3,386,1]{1,2,0:T(1,128)}, u32[]{:S(2)}, u32[]{:S(2)}) collective-permute-start(f32[3,386,1]{1,2,0:T(1,128)} %copy.24), channel_id=1, source_target_pairs={{0,1},{1,2},{2,3},{4,5},{5,6},{6,7},{8,9},{9,10},{10,11},{12,13},{... | collective-permute-start | bytes 13904 | tf_op jit(solution)/shard_map/ppermute | solution.py:25
  219.6 4.0 %collective-permute-start.17 = (f32[3,386,1]{1,2,0:T(1,128)}, f32[3,386,1]{1,2,0:T(1,128)}, u32[]{:S(2)}, u32[]{:S(2)}) collective-permute-start(f32[3,386,1]{1,2,0:T(1,128)} %copy.26), channel_id=1, source_target_pairs={{1,0},{2,1},{3,2},{5,4},{6,5},{7,6},{9,8},{10,9},{11,10},{13,12},{... | collective-permute-start | bytes 13904 | tf_op jit(solution)/shard_map/ppermute | solution.py:26
  229.3 3.2 collective-permute-start.18
  231.3 5.5 %collective-permute-start.19 = (f32[3,1,384]{2,1,0:T(1,128)S(1)}, f32[3,1,384]{2,1,0:T(1,128)S(1)}, u32[]{:S(2)}, u32[]{:S(2)}) collective-permute-start(f32[3,1,384]{2,1,0:T(1,128)S(1)} %get-tuple-element.30), channel_id=1, source_target_pairs={{4,0},{8,4},{12,8},{5,1},{9,5},{13,9},{6,2},{10,6},{14,10},{7,3},{... | collective-permute-start | bytes 13832 | tf_op jit(solution)/shard_map/ppermute | solution.py:26
  240.1 6.6 %collective-permute-start.20 = (f32[3,386,1]{1,2,0:T(1,128)}, f32[3,386,1]{1,2,0:T(1,128)}, u32[]{:S(2)}, u32[]{:S(2)}) collective-permute-start(f32[3,386,1]{1,2,0:T(1,128)} %copy.28), channel_id=1, source_target_pairs={{0,1},{1,2},{2,3},{4,5},{5,6},{6,7},{8,9},{9,10},{10,11},{12,13},{... | collective-permute-start | bytes 13904 | tf_op jit(solution)/shard_map/ppermute | solution.py:25
  245.4 4.0 %collective-permute-start.21 = (f32[3,386,1]{1,2,0:T(1,128)}, f32[3,386,1]{1,2,0:T(1,128)}, u32[]{:S(2)}, u32[]{:S(2)}) collective-permute-start(f32[3,386,1]{1,2,0:T(1,128)} %copy.30), channel_id=1, source_target_pairs={{1,0},{2,1},{3,2},{5,4},{6,5},{7,6},{9,8},{10,9},{11,10},{13,12},{... | collective-permute-start | bytes 13904 | tf_op jit(solution)/shard_map/ppermute | solution.py:26
  255.1 3.5 %collective-permute-start.22 = (f32[3,1,384]{2,1,0:T(1,128)S(1)}, f32[3,1,384]{2,1,0:T(1,128)S(1)}, u32[]{:S(2)}, u32[]{:S(2)}) collective-permute-start(f32[3,1,384]{2,1,0:T(1,128)S(1)} %get-tuple-element.27), channel_id=1, source_target_pairs={{0,4},{4,8},{8,12},{1,5},{5,9},{9,13},{2,6},{6,10},{10,14},{3,7},{... | collective-permute-start | bytes 13832 | tf_op jit(solution)/shard_map/ppermute | solution.py:25
  257.0 5.5 %collective-permute-start.23 = (f32[3,1,384]{2,1,0:T(1,128)S(1)}, f32[3,1,384]{2,1,0:T(1,128)S(1)}, u32[]{:S(2)}, u32[]{:S(2)}) collective-permute-start(f32[3,1,384]{2,1,0:T(1,128)S(1)} %get-tuple-element.28), channel_id=1, source_target_pairs={{4,0},{8,4},{12,8},{5,1},{9,5},{13,9},{6,2},{10,6},{14,10},{7,3},{... | collective-permute-start | bytes 13832 | tf_op jit(solution)/shard_map/ppermute | solution.py:26
  265.8 6.6 %collective-permute-start.24 = (f32[3,386,1]{1,2,0:T(1,128)}, f32[3,386,1]{1,2,0:T(1,128)}, u32[]{:S(2)}, u32[]{:S(2)}) collective-permute-start(f32[3,386,1]{1,2,0:T(1,128)} %copy.32), channel_id=1, source_target_pairs={{0,1},{1,2},{2,3},{4,5},{5,6},{6,7},{8,9},{9,10},{10,11},{12,13},{... | collective-permute-start | bytes 13904 | tf_op jit(solution)/shard_map/ppermute | solution.py:25
  271.2 4.0 %collective-permute-start.25 = (f32[3,386,1]{1,2,0:T(1,128)}, f32[3,386,1]{1,2,0:T(1,128)}, u32[]{:S(2)}, u32[]{:S(2)}) collective-permute-start(f32[3,386,1]{1,2,0:T(1,128)} %copy.34), channel_id=1, source_target_pairs={{1,0},{2,1},{3,2},{5,4},{6,5},{7,6},{9,8},{10,9},{11,10},{13,12},{... | collective-permute-start | bytes 13904 | tf_op jit(solution)/shard_map/ppermute | solution.py:26
  282.8 5.5 %collective-permute-start.27 = (f32[3,1,384]{2,1,0:T(1,128)S(1)}, f32[3,1,384]{2,1,0:T(1,128)S(1)}, u32[]{:S(2)}, u32[]{:S(2)}) collective-permute-start(f32[3,1,384]{2,1,0:T(1,128)S(1)} %get-tuple-element.26), channel_id=1, source_target_pairs={{4,0},{8,4},{12,8},{5,1},{9,5},{13,9},{6,2},{10,6},{14,10},{7,3},{... | collective-permute-start | bytes 13832 | tf_op jit(solution)/shard_map/ppermute | solution.py:26
  288.8 4.4 %collective-permute-start.28 = (f32[3,386,1]{1,2,0:T(1,128)S(1)}, f32[3,386,1]{1,2,0:T(1,128)S(1)}, u32[]{:S(2)}, u32[]{:S(2)}) collective-permute-start(f32[3,386,1]{1,2,0:T(1,128)S(1)} %copy.36), channel_id=1, source_target_pairs={{0,1},{1,2},{2,3},{4,5},{5,6},{6,7},{8,9},{9,10},{10,11},{12,13},{... | collective-permute-start | bytes 13904 | tf_op jit(solution)/shard_map/ppermute | solution.py:25
  291.9 4.2 %collective-permute-start.29 = (f32[3,386,1]{1,2,0:T(1,128)S(1)}, f32[3,386,1]{1,2,0:T(1,128)S(1)}, u32[]{:S(2)}, u32[]{:S(2)}) collective-permute-start(f32[3,386,1]{1,2,0:T(1,128)S(1)} %copy.38), channel_id=1, source_target_pairs={{1,0},{2,1},{3,2},{5,4},{6,5},{7,6},{9,8},{10,9},{11,10},{13,12},{... | collective-permute-start | bytes 13904 | tf_op jit(solution)/shard_map/ppermute | solution.py:26
  304.5 5.5 %collective-permute-start.31 = (f32[3,1,384]{2,1,0:T(1,128)S(1)}, f32[3,1,384]{2,1,0:T(1,128)S(1)}, u32[]{:S(2)}, u32[]{:S(2)}) collective-permute-start(f32[3,1,384]{2,1,0:T(1,128)S(1)} %get-tuple-element.24), channel_id=1, source_target_pairs={{4,0},{8,4},{12,8},{5,1},{9,5},{13,9},{6,2},{10,6},{14,10},{7,3},{... | collective-permute-start | bytes 13832 | tf_op jit(solution)/shard_map/ppermute | solution.py:26
  313.1 6.7 %collective-permute-start.32 = (f32[3,386,1]{1,2,0:T(1,128)}, f32[3,386,1]{1,2,0:T(1,128)}, u32[]{:S(2)}, u32[]{:S(2)}) collective-permute-start(f32[3,386,1]{1,2,0:T(1,128)} %copy.40), channel_id=1, source_target_pairs={{0,1},{1,2},{2,3},{4,5},{5,6},{6,7},{8,9},{9,10},{10,11},{12,13},{... | collective-permute-start | bytes 13904 | tf_op jit(solution)/shard_map/ppermute | solution.py:25
  318.5 3.8 %collective-permute-start.33 = (f32[3,386,1]{1,2,0:T(1,128)}, f32[3,386,1]{1,2,0:T(1,128)}, u32[]{:S(2)}, u32[]{:S(2)}) collective-permute-start(f32[3,386,1]{1,2,0:T(1,128)} %copy.42), channel_id=1, source_target_pairs={{1,0},{2,1},{3,2},{5,4},{6,5},{7,6},{9,8},{10,9},{11,10},{13,12},{... | collective-permute-start | bytes 13904 | tf_op jit(solution)/shard_map/ppermute | solution.py:26
  (26 other events, 366.4 us)
Sparse Core Ops, SparseCore 0:
  35.6 88.8 all-reduce.1
where the time goes:
time: 340 us; the launch traced here: 336 us
  waiting for transfers between devices  131 us (39%)
  starting transfers between devices  72.2 us (21%)
  local copies, waits for them, and re-layouts  55.9 us (16%)
  other arithmetic  53.1 us (16%)
  between operations  14.1 us (4%)
  matrix products  9.52 us (3%)
    psum x1, waiting for transfers between devices, body(): spectral = lax.psum(partial_modes, ('row', 'col'))  88.9 us
    ppermute x16, starting transfers between devices, with_halo(): before = lax.ppermute(last, axis, up)  43.4 us
    ppermute x16, waiting for transfers between devices, with_halo(): after = lax.ppermute(first, axis, down)  41.9 us
    div x8, other arithmetic, body(): stitched = (source + neighbour_sum(padded)) / denominator  34.2 us
    ppermute x16, starting transfers between devices, with_halo(): after = lax.ppermute(first, axis, down)  21 us
    ppermute x8, local copies, waits for them, and re-layouts, with_halo(): after = lax.ppermute(first, axis, down)  13.1 us
    slice x16, local copies, waits for them, and re-layouts, with_halo(): last = lax.slice_in_dim(x, length - width, length, axis=dim)  12.8 us
    ppermute x8, local copies, waits for them, and re-layouts, with_halo(): before = lax.ppermute(last, axis, up)  12.4 us
  transfers between devices with their start and end apart: 35, of which 17 were waited for; matrix products, arithmetic and copies ran while one was open for 9% of the time, Pallas kernels for 0%

commit v1 on v0

v1 whole, which is shorter than its diff:
```python
import functools
import math

import jax
import jax.numpy as jnp
import ml_dtypes
import numpy as np
from jax import lax
from jax.experimental import pallas as pl
from jax.experimental.pallas import tpu as pltpu
from jax.sharding import PartitionSpec as P

M = 128
SWEEPS = 8
LANES = 128
PAD = 16
MESH = pl.DeviceIdType.MESH
F32 = jnp.float32
BF16 = jnp.bfloat16


def np_split(x):
    hi = x.astype(np.float32).astype(ml_dtypes.bfloat16)
    lo = (x - hi.astype(np.float64)).astype(np.float32).astype(ml_dtypes.bfloat16)
    return hi, lo


def np_tables(count):
    k = np.arange(M)
    i = np.arange(count)
    scale = np.where(k == 0, math.sqrt(1.0 / count), math.sqrt(2.0 / count))
    cos = scale * np.cos(np.pi / (2 * count) * ((k * (2 * i[:, None] + 1)) % (4 * count)))
    sin = (
        -2.0
        * scale
        * np.sin(np.pi * k / (2 * count))
        * np.sin(np.pi / count * ((k * (i[:, None] + 1)) % (2 * count)))
    )
    eigen = 2.0 - 2.0 * np.cos(np.pi * k / count)
    return cos, sin, eigen


def split(x):
    hi = x.astype(BF16)
    return hi, (x - hi.astype(F32)).astype(BF16)


def iota(shape, dim):
    return lax.broadcasted_iota(jnp.int32, shape, dim)


def first_kernel(
    dims,
    gx_ref, gy_ref, mask_ref, off_ref, ty_hbm, tx_hbm,
    ts_ref, sp_ref,
    E, S, XA, XB, inv, ty, tx, part, pack, cols, r1, acc, r2, fin, acc2,
    tab_sem, cs_send, cs_recv, rs_send, rs_recv,
    p1s, p1r, p2s, p2r, p3s, p3r, p4s, p4r,
):
    R, C, CH, TH, TW, screen = dims
    W = TW + LANES
    half = TH // 2
    group = lax.axis_index("groups")
    row = lax.axis_index("row")
    col = lax.axis_index("col")
    modes = CH * M
    crows = modes // C
    nparts = min(R, crows // 8)
    prow = crows // nparts

    def at(r, c):
        return (group, r, c)

    ty_copy = pltpu.make_async_copy(ty_hbm.at[pl.ds(col * TW, TW)], ty, tab_sem.at[0])
    tx_copy = pltpu.make_async_copy(tx_hbm.at[row], tx, tab_sem.at[1])
    ty_copy.start()
    tx_copy.start()

    cols[...] = jnp.zeros_like(cols)
    E[:, 0:PAD, :] = jnp.zeros((2 * CH, PAD, W), F32)
    E[:, PAD + TH :, :] = jnp.zeros((2 * CH, PAD, W), F32)

    barrier = pltpu.get_barrier_semaphore()
    for off in range(1, C):
        pl.semaphore_signal(
            barrier, inc=1, device_id=at(row, lax.rem(col + off, C)), device_id_type=MESH
        )
    for off in range(1, R):
        pl.semaphore_signal(
            barrier, inc=1, device_id=at(lax.rem(row + off, R), col), device_id_type=MESH
        )

    here = 0.25 * off_ref[0 * R * C + row * C + col].astype(F32)
    below_row = jnp.minimum(row + 1, R - 1)
    right_col = jnp.minimum(col + 1, C - 1)
    stepx, stepy = [], []
    for c in range(CH):
        here = 0.25 * off_ref[c * R * C + row * C + col].astype(F32)
        stepx.append(0.25 * off_ref[c * R * C + below_row * C + col].astype(F32) - here)
        stepy.append(0.25 * off_ref[c * R * C + row * C + right_col].astype(F32) - here)
    ER = 32

    def edge_rows(t, carry):
        r0 = pl.multiple_of(t * ER, ER)
        rows = iota((ER, 1), 0) + r0
        lanes = iota((1, TW), 1)
        damp = 1.0 - 0.75 * mask_ref[pl.ds(r0, ER), :].astype(F32)
        last_row = (rows == TH - 1).astype(F32)
        last_col = (lanes == TW - 1).astype(F32)
        keep_row = jnp.where((rows == TH - 1) & (row == R - 1), 0.0, 1.0)
        keep_col = jnp.where((lanes == TW - 1) & (col == C - 1), 0.0, 1.0)
        b0 = pl.multiple_of(r0 + PAD, 8)
        for c in range(CH):
            ex = (gx_ref[c, pl.ds(r0, ER), :].astype(F32) * damp + last_row * stepx[c]) * keep_row
            ey = (gy_ref[c, pl.ds(r0, ER), :].astype(F32) * damp + last_col * stepy[c]) * keep_col
            E[c, pl.ds(b0, ER), 0:TW] = ex
            E[CH + c, pl.ds(b0, ER), 0:TW] = ey
        return carry

    lax.fori_loop(0, TH // ER, edge_rows, 0)

    lane = iota((half, LANES), 1)
    for side in range(2):
        total = jnp.zeros((half, LANES), F32)
        for h in range(2):
            for a in range(2 * CH):
                rows = slice(PAD + h * half, PAD + (h + 1) * half)
                tile = slice(TW - LANES, TW) if side == 0 else slice(0, LANES)
                spot = 8 * a + 64 * h
                shift = (spot + (8 if side == 0 else 0)) % LANES
                x = E[a, rows, tile]
                if shift:
                    x = pltpu.roll(x, shift, 1)
                total = jnp.where((lane >= spot) & (lane < spot + 8), x, total)
        pack[side] = total

    pl.semaphore_wait(barrier, C - 1 + R - 1)
    to_right = pltpu.make_async_remote_copy(
        src_ref=pack.at[0], dst_ref=cols.at[0], send_sem=cs_send.at[0], recv_sem=cs_recv.at[0],
        device_id=at(row, jnp.minimum(col + 1, C - 1)), device_id_type=MESH,
    )
    to_left = pltpu.make_async_remote_copy(
        src_ref=pack.at[1], dst_ref=cols.at[1], send_sem=cs_send.at[1], recv_sem=cs_recv.at[1],
        device_id=at(row, jnp.maximum(col - 1, 0)), device_id_type=MESH,
    )
    pl.when(col < C - 1)(to_right.start)
    pl.when(col > 0)(to_left.start)

    IR = 32
    def inv_rows(t, carry):
        r0 = pl.multiple_of(t * IR, IR)
        places = iota((IR, 1), 0) + r0 - PAD + row * TH
        lanes = iota((1, W), 1)
        lanes = jnp.where(lanes < TW + 8, lanes, lanes - W) + col * TW
        crow = (places > 0).astype(F32) + (places < R * TH - 1).astype(F32)
        ccol = (lanes > 0).astype(F32) + (lanes < C * TW - 1).astype(F32)
        inside = ((places >= 0) & (places < R * TH)).astype(F32) * (
            (lanes >= 0) & (lanes < C * TW)
        ).astype(F32)
        inv[pl.ds(r0, IR), :] = inside / (screen + crow + ccol)
        return carry

    lax.fori_loop(0, (TH + 2 * PAD) // IR, inv_rows, 0)

    ty_copy.wait()
    tx_copy.wait()
    for c in range(CH):
        hs = []
        for d in range(2):
            e = E[d * CH + c, PAD : PAD + TH, 0:TW].astype(BF16)
            h = jnp.dot(e, ty[:, d * 2 * M : (d + 1) * 2 * M], preferred_element_type=F32)
            hs.append(h[:, :M] + h[:, M:])
        h = jnp.concatenate(hs, axis=0)
        hi, lo = split(h)
        o = jnp.dot(tx[...], jnp.concatenate([hi, lo], axis=1), preferred_element_type=F32)
        part[c * M : (c + 1) * M, :] = (o[:M, :M] + o[M:, :M]) + (o[:M, M:] + o[M:, M:])

    p1 = []
    for off in range(1, C):
        d = lax.rem(col + off, C)
        cp = pltpu.make_async_remote_copy(
            src_ref=part.at[pl.ds(pl.multiple_of(d * crows, 8), crows)], dst_ref=r1.at[off],
            send_sem=p1s.at[off], recv_sem=p1r.at[off],
            device_id=at(row, d), device_id_type=MESH,
        )
        cp.start()
        p1.append(cp)

    pl.when(col > 0)(to_right.wait_recv)
    pl.when(col < C - 1)(to_left.wait_recv)
    for a in range(2 * CH):
        for h in range(2):
            rows = slice(PAD + h * half, PAD + (h + 1) * half)
            spot = 8 * a + 64 * h
            left = pltpu.roll(cols[0], (120 - spot) % LANES, 1)
            right = cols[1]
            if spot:
                right = pltpu.roll(right, LANES - spot, 1)
            E[a, rows, TW:W] = jnp.where(lane < 8, right, jnp.where(lane >= 120, left, 0.0))
    to_below = pltpu.make_async_remote_copy(
        src_ref=E.at[:, pl.ds(PAD + TH - 8, 8), :], dst_ref=E.at[:, pl.ds(PAD - 8, 8), :],
        send_sem=rs_send.at[0], recv_sem=rs_recv.at[0],
        device_id=at(jnp.minimum(row + 1, R - 1), col), device_id_type=MESH,
    )
    to_above = pltpu.make_async_remote_copy(
        src_ref=E.at[:, pl.ds(PAD, 8), :], dst_ref=E.at[:, pl.ds(PAD + TH, 8), :],
        send_sem=rs_send.at[1], recv_sem=rs_recv.at[1],
        device_id=at(jnp.maximum(row - 1, 0), col), device_id_type=MESH,
    )
    pl.when(row < R - 1)(to_below.start)
    pl.when(row > 0)(to_above.start)

    for cp in p1:
        cp.wait_recv()
    total = part[pl.ds(pl.multiple_of(col * crows, 8), crows), :]
    for off in range(1, C):
        total = total + r1[off]
    acc[...] = total

    def guarded(cond, f):
        if nparts == R:
            f()
        else:
            pl.when(cond)(f)

    p2 = []
    for off in range(1, R):
        d = lax.rem(row + off, R)
        dd = jnp.minimum(d, nparts - 1) if nparts < R else d
        cp = pltpu.make_async_remote_copy(
            src_ref=acc.at[pl.ds(pl.multiple_of(dd * prow, 8), prow)], dst_ref=r2.at[off],
            send_sem=p2s.at[off], recv_sem=p2r.at[off],
            device_id=at(d, col), device_id_type=MESH,
        )
        guarded(d < nparts, cp.start)
        p2.append((cp, d))

    pl.when(row > 0)(to_below.wait_recv)
    pl.when(row < R - 1)(to_above.wait_recv)
    HR = 40
    nchunk = (TH + 16) // HR

    XA[:, 0:8, :] = jnp.zeros((CH, 8, W), F32)
    XA[:, PAD + TH + 8 :, :] = jnp.zeros((CH, 8, W), F32)
    XB[:, 0:8, :] = jnp.zeros((CH, 8, W), F32)
    XB[:, PAD + TH + 8 :, :] = jnp.zeros((CH, 8, W), F32)

    def source_rows(t, carry):
        b0 = pl.multiple_of(8 + t * HR, 8)
        d = inv[pl.ds(b0, HR), :]
        for c in range(CH):
            wide = E[c, pl.ds(pl.multiple_of(b0 - 8, 8), HR + 8), :]
            ey = E[CH + c, pl.ds(b0, HR), :]
            s = (wide[7 : 7 + HR] - wide[8:]) + (pltpu.roll(ey, 1, 1) - ey)
            s = s * d
            S[c, pl.ds(b0, HR), :] = s
            XA[c, pl.ds(b0, HR), :] = s
        return carry

    lax.fori_loop(0, nchunk, source_rows, 0)

    def sweep(src, dst):
        def rows(t, carry):
            b0 = pl.multiple_of(8 + t * HR, 8)
            d = inv[pl.ds(b0, HR), :]
            for c in range(CH):
                wide = src[c, pl.ds(pl.multiple_of(b0 - 8, 8), HR + 16), :]
                mid = wide[8 : 8 + HR]
                nb = (wide[7 : 7 + HR] + wide[9 : 9 + HR]) + (
                    pltpu.roll(mid, 1, 1) + pltpu.roll(mid, W - 1, 1)
                )
                dst[c, pl.ds(b0, HR), :] = S[c, pl.ds(b0, HR), :] + nb * d
            return carry

        lax.fori_loop(0, nchunk, rows, 0)

    sweep(XA, XB)
    sweep(XB, XA)

    for cp, d in p2:
        guarded(row < nparts, cp.wait_recv)
    me = jnp.minimum(row, nparts - 1) if nparts < R else row
    mine = pl.ds(pl.multiple_of(me * prow, 8), prow)

    def sum_rows():
        total = acc[mine, :]
        for off in range(1, R):
            total = total + r2[off]
        fin[...] = total
        acc2[mine, :] = total

    guarded(row < nparts, sum_rows)
    p3 = []
    for off in range(1, R):
        d = lax.rem(row + off, R)
        s = lax.rem(row + R - off, R)
        cp = pltpu.make_async_remote_copy(
            src_ref=fin, dst_ref=acc2.at[mine],
            send_sem=p3s.at[off], recv_sem=p3r.at[off],
            device_id=at(d, col), device_id_type=MESH,
        )
        guarded(row < nparts, cp.start)
        p3.append((cp, s))

    sweep(XA, XB)
    sweep(XB, XA)

    for cp, s in p3:
        guarded(s < nparts, cp.wait_recv)
    own = pl.ds(pl.multiple_of(col * crows, 8), crows)
    p4 = []
    for off in range(1, C):
        d = lax.rem(col + off, C)
        cp = pltpu.make_async_remote_copy(
            src_ref=acc2, dst_ref=sp_ref.at[own],
            send_sem=p4s.at[off], recv_sem=p4r.at[off],
            device_id=at(row, d), device_id_type=MESH,
        )
        cp.start()
        p4.append(cp)
    sp_ref[own, :] = acc2[...]

    sweep(XA, XB)
    sweep(XB, XA)
    LR = 32

    def last_rows(t, carry):
        b0 = pl.multiple_of(PAD + t * LR, 8)
        o0 = pl.multiple_of(t * LR, 8)
        d = inv[pl.ds(b0, LR), 0:TW]
        for c in range(CH):
            wide = XA[c, pl.ds(pl.multiple_of(b0 - 8, 8), LR + 16), :]
            mid = wide[8 : 8 + LR]
            side = pltpu.roll(mid, 1, 1) + pltpu.roll(mid, W - 1, 1)
            nb = (wide[7 : 7 + LR] + wide[9 : 9 + LR])[:, 0:TW] + side[:, 0:TW]
            ts_ref[c, pl.ds(o0, LR), :] = S[c, pl.ds(b0, LR), 0:TW] + nb * d
        return carry

    lax.fori_loop(0, TH // LR, last_rows, 0)

    for cp in p4:
        cp.wait_recv()
    pl.when(col < C - 1)(to_right.wait_send)
    pl.when(col > 0)(to_left.wait_send)
    pl.when(row < R - 1)(to_below.wait_send)
    pl.when(row > 0)(to_above.wait_send)
    for cp in p1:
        cp.wait_send()
    for cp, d in p2:
        guarded(d < nparts, cp.wait_send)
    for cp, d in p3:
        guarded(row < nparts, cp.wait_send)
    for cp in p4:
        cp.wait_send()


def last_kernel(
    dims,
    pos_ref, sp_ref, ts_ref, tb_ref, mu_ref, cxk_ref, cxr_ref, cyb_ref, cys_ref, cyk_ref,
    out_ref, H,
):
    R, C, CH, TH, TW, screen = dims
    W = TW + LANES
    highest = lax.Precision.HIGHEST
    row, col = pos_ref[0], pos_ref[1]
    top, bottom = row == 0, row == R - 1
    left, right = col == 0, col == C - 1
    sp = sp_ref[...]
    coeffs = sp * tb_ref[0]
    moved = sp * tb_ref[1]

    hi, lo = split(moved)
    both = jnp.concatenate([hi, lo], axis=1)
    h = jnp.dot(cxr_ref[...], jnp.concatenate([both, both], axis=0), preferred_element_type=F32)
    H[...] = h[:, :M] + h[:, M:]

    @pl.when(top | bottom)
    def _():
        strip = jnp.where(top, 1, 0)
        tab = cxk_ref[...]
        lanes = jnp.where(top, 0.0, 1.0)
        first, last = tab[:, 0:LANES], tab[:, TW - LANES : TW]
        pick = jnp.where(top, first, last)
        u = lax.dot_general(
            pick, coeffs, (((0,), (0,)), ((), ())), precision=highest, preferred_element_type=F32
        )
        u = jnp.where(top, u[0:16], u[LANES - 16 :])
        r = iota((16, M), 0)
        edge = (top & (r == 0)) | (bottom & (r == 15))
        scale = 1.0 / (screen + jnp.where(edge, 3.0, 4.0))
        own = 2.0 - mu_ref[...]
        for _ in range(SWEEPS):
            up = jnp.where(r == 0, 0.0, pltpu.roll(u, 1, 0))
            down = jnp.where(r == 15, 0.0, pltpu.roll(u, 15, 0))
            u = (up + down + own * u) * scale

        @pl.when(top)
        def _():
            H[0:8, :] = u[0:8]

        @pl.when(bottom)
        def _():
            H[TH - 8 : TH, :] = u[8:16]

    hh, hl = split(H[...])
    lhs = jnp.concatenate([hh, hl, hh], axis=1)
    out_ref[0] = jnp.dot(lhs, cyb_ref[...], preferred_element_type=F32) + ts_ref[0]

    @pl.when(left | right)
    def _():
        cy = jnp.where(left, cys_ref[0:16, :], cys_ref[TW - 16 : TW, :])
        z = lax.dot_general(
            cy, coeffs, (((1,), (1,)), ((), ())), precision=highest, preferred_element_type=F32
        )
        w = jnp.dot(z, cxk_ref[...], precision=highest, preferred_element_type=F32)
        r = iota((16, W), 0)
        lanes = iota((16, W), 1)
        place = jnp.where(lanes < TW + 8, lanes, lanes - W) + row * TH
        inside = (place >= 0) & (place < R * TH)
        cx = (place > 0).astype(F32) + (place < R * TH - 1).astype(F32)
        edge = (left & (r == 0)) | (right & (r == 15))
        scale = jnp.where(inside, 1.0, 0.0) / (screen + cx + jnp.where(edge, 1.0, 2.0))
        w = jnp.where(inside, w, 0.0)
        for _ in range(SWEEPS):
            up = jnp.where(r == 0, 0.0, pltpu.roll(w, 1, 0))
            down = jnp.where(r == 15, 0.0, pltpu.roll(w, 15, 0))
            w = (up + down + (pltpu.roll(w, 1, 1) + pltpu.roll(w, W - 1, 1))) * scale
        wide = jnp.concatenate(
            [w[:, 0:TW], jnp.zeros((LANES - 16, TW), F32)], axis=0
        )
        wt = wide.T
        lane = iota((TW, LANES), 1)

        @pl.when(left)
        def _():
            ts = ts_ref[0, :, 0:LANES]
            out_ref[0, :, 0:LANES] = jnp.where(lane < 8, wt + ts, out_ref[0, :, 0:LANES])

        @pl.when(right)
        def _():
            ts = ts_ref[0, :, TW - LANES : TW]
            turned = pltpu.roll(wt, LANES - 16, 1)
            out_ref[0, :, TW - LANES : TW] = jnp.where(
                lane >= LANES - 8, turned + ts, out_ref[0, :, TW - LANES : TW]
            )


def body(grad_x, grad_y, seam_mask, tile_offset, tables):
    CH, TH, TW = grad_x.shape
    R = lax.axis_size("row")
    C = lax.axis_size("col")
    NX, NY = TH * R, TW * C
    screen = 0.5 * math.pi * math.pi / (NX * NY)
    dims = (R, C, CH, TH, TW, screen)
    W = TW + LANES
    modes = CH * M
    crows = modes // C
    nparts = min(R, crows // 8)
    prow = crows // nparts
    ty, tx, tb, mu, cxk, cxr, cyb, cys, cyk = tables
    vmem = pl.BlockSpec(memory_space=pltpu.VMEM)
    smem = pl.BlockSpec(memory_space=pltpu.SMEM)
    anys = pl.BlockSpec(memory_space=pl.ANY)
    rows = TH + 2 * PAD
    dma = pltpu.SemaphoreType.DMA
    ts, sp = pl.pallas_call(
        functools.partial(first_kernel, dims),
        out_shape=(
            jax.ShapeDtypeStruct((CH, TH, TW), F32),
            jax.ShapeDtypeStruct((modes, M), F32),
        ),
        in_specs=[vmem, vmem, vmem, smem, anys, anys],
        out_specs=(vmem, vmem),
        scratch_shapes=[
            pltpu.VMEM((2 * CH, rows, W), F32),
            pltpu.VMEM((CH, rows, W), F32),
            pltpu.VMEM((CH, rows, W), F32),
            pltpu.VMEM((CH, rows, W), F32),
            pltpu.VMEM((rows, W), F32),
            pltpu.VMEM((TW, 4 * M), BF16),
            pltpu.VMEM((2 * M, 2 * TH), BF16),
            pltpu.VMEM((modes, M), F32),
            pltpu.VMEM((2, TH // 2, LANES), F32),
            pltpu.VMEM((2, TH // 2, LANES), F32),
            pltpu.VMEM((C, crows, M), F32),
            pltpu.VMEM((crows, M), F32),
            pltpu.VMEM((R, prow, M), F32),
            pltpu.VMEM((prow, M), F32),
            pltpu.VMEM((crows, M), F32),
            dma((2,)), dma((2,)), dma((2,)), dma((2,)), dma((2,)),
            dma((C,)), dma((C,)), dma((R,)), dma((R,)),
            dma((R,)), dma((R,)), dma((C,)), dma((C,)),
        ],
        compiler_params=pltpu.CompilerParams(
            collective_id=0, has_side_effects=True, vmem_limit_bytes=48 * 2**20
        ),
        name="sums_and_sweeps",
    )(grad_x, grad_y, seam_mask, tile_offset.reshape(-1), ty, tx)

    pos = jnp.stack([lax.axis_index("row"), lax.axis_index("col")]).astype(jnp.int32)
    here = lambda i, p: (p[0], 0)
    spec = pltpu.PrefetchScalarGridSpec(
        num_scalar_prefetch=1,
        grid=(CH,),
        in_specs=[
            pl.BlockSpec((M, M), lambda i, p: (i, 0)),
            pl.BlockSpec((1, TH, TW), lambda i, p: (i, 0, 0)),
            pl.BlockSpec((2, M, M), lambda i, p: (0, 0, 0)),
            pl.BlockSpec((1, M), lambda i, p: (0, 0)),
            pl.BlockSpec((M, W), lambda i, p: (p[0], 0)),
            pl.BlockSpec((TH, 2 * M), lambda i, p: (p[0], 0)),
            pl.BlockSpec((3 * M, TW), lambda i, p: (0, p[1])),
            pl.BlockSpec((TW, M), lambda i, p: (p[1], 0)),
            pl.BlockSpec((8, LANES), lambda i, p: (0, 0)),
        ],
        out_specs=pl.BlockSpec((1, TH, TW), lambda i, p: (i, 0, 0)),
        scratch_shapes=[pltpu.VMEM((TH, M), F32)],
    )
    return pl.pallas_call(
        functools.partial(last_kernel, dims),
        grid_spec=spec,
        out_shape=jax.ShapeDtypeStruct((CH, TH, TW), F32),
        compiler_params=pltpu.CompilerParams(vmem_limit_bytes=40 * 2**20),
        name="synthesis",
    )(pos, sp, ts, tb, mu, cxk, cxr, cyb, cys, cyk)


def solution(mesh):
    in_specs = (
        P(None, ("groups", "row"), "col"),
        P(None, ("groups", "row"), "col"),
        P(("groups", "row"), "col"),
        P(None, "groups", None),
        P(),
    )
    out_specs = P(None, ("groups", "row"), "col")
    R, C = mesh.shape["row"], mesh.shape["col"]
    G = mesh.shape["groups"]

    def whole(grad_x, grad_y, seam_mask, tile_offset):
        NX, NY = grad_x.shape[1] // G, grad_x.shape[2]
        TH, TW = NX // R, NY // C
        W = TH + LANES
        screen = 0.5 * math.pi * math.pi / (NX * NY)
        cx, sx, ex = np_tables(NX)
        cy, sy, ey = np_tables(NY)
        ty = np.concatenate(np_split(cy) + np_split(sy), axis=1)
        tiles = [
            np.concatenate([sx[r * TH : (r + 1) * TH].T, cx[r * TH : (r + 1) * TH].T], axis=1)
            for r in range(R)
        ]
        tx = np.stack([np.concatenate(np_split(t), axis=0) for t in tiles])
        lam = ex[:, None] + ey[None, :]
        tb = np.stack([1.0 / (screen + lam), ((4.0 - lam) / (4.0 + screen)) ** SWEEPS / (screen + lam)])
        cxk = np.zeros((R, M, W))
        for r in range(R):
            cxk[r, :, :TH] = cx[r * TH : (r + 1) * TH].T
            if r > 0:
                cxk[r, :, W - 8 :] = cx[r * TH - 8 : r * TH].T
            if r < R - 1:
                cxk[r, :, TH : TH + 8] = cx[(r + 1) * TH : (r + 1) * TH + 8].T
        cxr = np.concatenate(np_split(cx), axis=1)
        hi, lo = np_split(cy.T)
        cyb = np.concatenate([hi, hi, lo], axis=0)
        tables = (
            jnp.asarray(ty), jnp.asarray(tx),
            jnp.asarray(tb.astype(np.float32)),
            jnp.asarray(ey[None, :].astype(np.float32)),
            jnp.asarray(cxk.reshape(R * M, W).astype(np.float32)),
            jnp.asarray(cxr), jnp.asarray(cyb),
            jnp.asarray(cy.astype(np.float32)),
            jnp.zeros((8, LANES), F32),
        )
        f = jax.shard_map(body, mesh=mesh, in_specs=in_specs, out_specs=out_specs, check_vma=False)
        return f(grad_x, grad_y, seam_mask, tile_offset, tables)

    return whole
```

time: 340 us -> 47.1 us (0.14); the launches traced: 336 us -> 46.8 us
  waiting for transfers between devices: 131 us -> 0 us
  starting transfers between devices: 72.2 us -> 0 us
  other arithmetic: 53.1 us -> 0.07 us
  local copies, waits for them, and re-layouts: 55.9 us -> 8.49 us
  Pallas kernels: 0 us -> 38.1 us
  between operations: 14.1 us -> 0.11 us
  matrix products: 9.52 us -> 0 us
    psum x1 -> x0, waiting for transfers between devices: 88.9 us -> none  [body(): spectral = lax.psum(partial_modes, ('row', 'col'))]
    ppermute x34 -> x0, starting transfers between devices: 72.2 us -> none  [the longest x16 43.4 us: with_halo(): before = lax.ppermute(last, axis, up)]
    ppermute x34 -> x0, waiting for transfers between devices: 42 us -> none  [the longest x16 41.9 us: with_halo(): after = lax.ppermute(first, axis, down)]
    pallas_call x0 -> x2, Pallas kernels: none -> 38.1 us  [the longest x1 30 us: body(): pl.pallas_call(functools.partial(first_kernel, dims), out_shape=(jax.Shap...]
    div x8 -> x0, other arithmetic: 34.2 us -> none  [body(): stitched = (source + neighbour_sum(padded)) / denominator]
    slice x27 -> x0, local copies, waits for them, and re-layouts: 28.5 us -> none  [the longest x16 12.8 us: with_halo(): last = lax.slice_in_dim(x, length - width, length, axis=dim)]
    ppermute x17 -> x0, local copies, waits for them, and re-layouts: 27.3 us -> none  [the longest x8 13.1 us: with_halo(): after = lax.ppermute(first, axis, down)]
    dot_general x4 -> x0, matrix products: 9.52 us -> none  [the longest x1 2.58 us: body(): halves = jnp.einsum('cij,lj->cil', source, table_y, precision=highest)]
  transfers between devices with their start and end apart: 35 -> 0, of which waited for: 17 -> 0; matrix products, arithmetic and copies ran while one was open for 9% -> 0% of each run, Pallas kernels for 0% -> 0%
where the time goes in v1:
time: 47.1 us; the launch traced here: 46.8 us
  Pallas kernels  38.1 us (81%)
  local copies, waits for them, and re-layouts  8.49 us (18%)
    pallas_call x1, Pallas kernels, body(): pl.pallas_call(functools.partial(first_kernel, dims), out_shape=(jax.Shap...  30 us
    pallas_call x1, Pallas kernels, body(): pl.pallas_call(functools.partial(last_kernel, dims), grid_spec=spec, out_...  8.16 us
    unnamed x24, local copies, waits for them, and re-layouts  7.71 us

profile of v1, /device:TPU:0, one launch (start us, length us, event | category | flops | bytes accessed | tf_op | source)
XLA Modules:
  0.0 46.8 jit_solution(6991111417640945981)
XLA Ops:
  0.0 0.1 pad_add_fusion.pos_ref
  0.1 0.8 %reshape.3.off_ref = s32[48]{0:T(128)S(1)} reshape(s32[3,4,4]{2,1,0:T(4,128)} %param.16) | data formatting | bytes 384 | tf_op jit(solution)/shard_map/reshape | solution.py:498
  0.9 0.0 copy-start.1
  0.9 1.4 %copy-done.1 = bf16[4,256,768]{2,1,0:T(8,128)(2,1)S(1)} copy-done((bf16[4,256,768]{2,1,0:T(8,128)(2,1)S(1)}, bf16[4,256,768]{2,1,0:T(8,128)(2,1)}, u32[]{:S(2)}) %copy-start.1) | copy-done | bytes 1572888
  2.3 0.0 copy-start.2
  2.3 1.4 %copy-done.2 = bf16[1536,512]{1,0:T(8,128)(2,1)S(1)} copy-done((bf16[1536,512]{1,0:T(8,128)(2,1)S(1)}, bf16[1536,512]{1,0:T(8,128)(2,1)}, u32[]{:S(2)}) %copy-start.2) | copy-done | bytes 1572888
  3.7 0.0 copy-start.5
  3.7 1.2 %copy-done.5 = bf16[3,384,384]{2,1,0:T(8,128)(2,1)S(1)} copy-done((bf16[3,384,384]{2,1,0:T(8,128)(2,1)S(1)}, bf16[3,384,384]{2,1,0:T(8,128)(2,1)}, u32[]{:S(2)}) %copy-start.5) | copy-done | bytes 884760
  4.8 0.0 copy-start.6
  4.8 1.2 %copy-done.6 = bf16[3,384,384]{2,1,0:T(8,128)(2,1)S(1)} copy-done((bf16[3,384,384]{2,1,0:T(8,128)(2,1)S(1)}, bf16[3,384,384]{2,1,0:T(8,128)(2,1)}, u32[]{:S(2)}) %copy-start.6) | copy-done | bytes 884760
  6.0 0.0 copy-start.9
  6.0 1.1 %copy-done.9 = s32[384,384]{1,0:T(8,128)S(1)} copy-done((s32[384,384]{1,0:T(8,128)S(1)}, s32[384,384]{1,0:T(8,128)}, u32[]{:S(2)}) %copy-start.9) | copy-done | bytes 589848
  7.1 0.0 copy-start.3
  7.1 0.0 copy-start.4
  7.1 0.0 copy-start.7
  7.1 0.0 copy-start.8
  7.1 0.0 copy-start.10
  7.1 0.0 copy-start.11
  7.1 30.0 %sums_and_sweeps.1 = (f32[3,384,384]{2,1,0:T(8,128)}, f32[384,128]{1,0:T(8,128)S(1)}) custom-call(bf16[3,384,384]{2,1,0:T(8,128)(2,1)S(1)} %copy-done.5, bf16[3,384,384]{2,1,0:T(8,128)(2,1)S(1)} %copy-done.6, s32[384,384]{1,0:T(8,128)S(1)} %copy-done.9, s32[48]{0:T(128)S(1)} %reshape.3.off_ref, bf16[1536,512]{1,0:T(8,128)(2,1)S(1)} %copy-done.2, ...), custom_call_target="tpu_custom_call" | custom-call | tf_op jit(solution)/shard_map/sums_and_sweeps/pallas_call | solution.py:466
  37.1 0.0 copy-done.3
  37.1 0.0 copy-done.4
  37.1 0.0 copy-done.7
  37.1 0.0 copy-done.8
  37.1 0.0 copy-done.10
  37.1 0.0 copy-done.11
  37.1 0.0 copy-start
  37.2 1.5 %copy-done = f32[3,384,384]{2,1,0:T(8,128)S(1)} copy-done((f32[3,384,384]{2,1,0:T(8,128)S(1)}, f32[3,384,384]{2,1,0:T(8,128)}, u32[]{:S(2)}) %copy-start) | copy-done | bytes 1769496
  38.6 8.2 %synthesis.1 = f32[3,384,384]{2,1,0:T(8,128)} custom-call(s32[2]{0:T(128)S(1)} %pad_add_fusion.pos_ref, f32[384,128]{1,0:T(8,128)S(1)} %get-tuple-element.7.sp_ref, f32[3,384,384]{2,1,0:T(8,128)S(1)} %copy-done, f32[2,128,128]{2,1,0:T(8,128)S(1)} %copy-done.10, f32[1,128]{1,0:T(1,128)S(1)} %copy-done.11, f32[512,512]{1,0:T(8,128)S(1)} %copy-done.4, ...), custom_call_target="tpu_custom_call" | custom-call | tf_op jit(solution)/shard_map/synthesis/pallas_call | solution.py:519
  (1 shorter events, 0.0 us)
Async XLA Ops:
  0.9 1.4 %copy-start.1 = (bf16[4,256,768]{2,1,0:T(8,128)(2,1)S(1)}, bf16[4,256,768]{2,1,0:T(8,128)(2,1)}, u32[]{:S(2)}) copy-start(bf16[4,256,768]{2,1,0:T(8,128)(2,1)} %constant.26.clone.tx_hbm) | copy-start | bytes 4718596
  2.3 1.4 %copy-start.2 = (bf16[1536,512]{1,0:T(8,128)(2,1)S(1)}, bf16[1536,512]{1,0:T(8,128)(2,1)}, u32[]{:S(2)}) copy-start(bf16[1536,512]{1,0:T(8,128)(2,1)} %constant.25.clone.ty_hbm) | copy-start | bytes 4718596
  3.7 1.2 %copy-start.5 = (bf16[3,384,384]{2,1,0:T(8,128)(2,1)S(1)}, bf16[3,384,384]{2,1,0:T(8,128)(2,1)}, u32[]{:S(2)}) copy-start(bf16[3,384,384]{2,1,0:T(8,128)(2,1)} %gx_ref.1) | copy-start | bytes 2654212
  4.8 1.2 %copy-start.6 = (bf16[3,384,384]{2,1,0:T(8,128)(2,1)S(1)}, bf16[3,384,384]{2,1,0:T(8,128)(2,1)}, u32[]{:S(2)}) copy-start(bf16[3,384,384]{2,1,0:T(8,128)(2,1)} %gy_ref.1) | copy-start | bytes 2654212
  6.0 1.1 %copy-start.9 = (s32[384,384]{1,0:T(8,128)S(1)}, s32[384,384]{1,0:T(8,128)}, u32[]{:S(2)}) copy-start(s32[384,384]{1,0:T(8,128)} %mask_ref.1) | copy-start | bytes 1769476
  7.1 30.0 %copy-start.3 = (bf16[384,1536]{1,0:T(8,128)(2,1)S(1)}, bf16[384,1536]{1,0:T(8,128)(2,1)}, u32[]{:S(2)}) copy-start(bf16[384,1536]{1,0:T(8,128)(2,1)} %constant.31.clone.cyb_ref) | copy-start | bytes 3538948
  7.1 30.0 %copy-start.4 = (f32[512,512]{1,0:T(8,128)S(1)}, f32[512,512]{1,0:T(8,128)}, u32[]{:S(2)}) copy-start(f32[512,512]{1,0:T(8,128)} %constant.29.clone.cxk_ref) | copy-start | bytes 3145732
  7.1 30.0 %copy-start.7 = (f32[1536,128]{1,0:T(8,128)S(1)}, f32[1536,128]{1,0:T(8,128)}, u32[]{:S(2)}) copy-start(f32[1536,128]{1,0:T(8,128)} %constant.32.clone.cys_ref) | copy-start | bytes 2359300
  7.1 30.0 %copy-start.8 = (bf16[1536,256]{1,0:T(8,128)(2,1)S(1)}, bf16[1536,256]{1,0:T(8,128)(2,1)}, u32[]{:S(2)}) copy-start(bf16[1536,256]{1,0:T(8,128)(2,1)} %constant.30.clone.cxr_ref) | copy-start | bytes 2359300
  7.1 30.0 %copy-start.10 = (f32[2,128,128]{2,1,0:T(8,128)S(1)}, f32[2,128,128]{2,1,0:T(8,128)}, u32[]{:S(2)}) copy-start(f32[2,128,128]{2,1,0:T(8,128)} %constant.27.clone.tb_ref) | copy-start | bytes 393220
  7.1 30.0 %copy-start.11 = (f32[1,128]{1,0:T(1,128)S(1)}, f32[1,128]{1,0:T(1,128)}, u32[]{:S(2)}) copy-start(f32[1,128]{1,0:T(1,128)} %constant.28.clone.mu_ref) | copy-start | bytes 1540
  37.1 1.5 %copy-start = (f32[3,384,384]{2,1,0:T(8,128)S(1)}, f32[3,384,384]{2,1,0:T(8,128)}, u32[]{:S(2)}) copy-start(f32[3,384,384]{2,1,0:T(8,128)} %get-tuple-element.8.ts_ref) | copy-start | bytes 5308420

commit v2 on v1

--- a/solution.py
+++ b/solution.py
@@ -51,14 +51,15 @@
 
 def first_kernel(
     dims,
-    gx_ref, gy_ref, mask_ref, off_ref, ty_hbm, tx_hbm,
+    gx_hbm, gy_hbm, mask_hbm, off_ref, ty_hbm, tx_hbm,
     ts_ref, sp_ref,
-    E, S, XA, XB, inv, ty, tx, part, pack, cols, r1, acc, r2, fin, acc2,
-    tab_sem, cs_send, cs_recv, rs_send, rs_recv,
+    gx_ref, gy_ref, mask_ref, E, S, XA, XB, inv, ty, tx, part, pack, cols, r1, acc, r2, fin, acc2,
+    in_sem, tab_sem, cs_send, cs_recv, rs_send, rs_recv,
     p1s, p1r, p2s, p2r, p3s, p3r, p4s, p4r,
 ):
     R, C, CH, TH, TW, screen = dims
     W = TW + LANES
+    Q = W // LANES
     half = TH // 2
     group = lax.axis_index("groups")
     row = lax.axis_index("row")
@@ -73,6 +74,14 @@
 
     ty_copy = pltpu.make_async_copy(ty_hbm.at[pl.ds(col * TW, TW)], ty, tab_sem.at[0])
     tx_copy = pltpu.make_async_copy(tx_hbm.at[row], tx, tab_sem.at[1])
+    loads = [
+        pltpu.make_async_copy(src, dst, in_sem.at[i])
+        for i, (src, dst) in enumerate(
+            ((mask_hbm, mask_ref), (gx_hbm, gx_ref), (gy_hbm, gy_ref))
+        )
+    ]
+    for cp in loads:
+        cp.start()
     ty_copy.start()
     tx_copy.start()
 
@@ -90,14 +99,13 @@
             barrier, inc=1, device_id=at(lax.rem(row + off, R), col), device_id_type=MESH
         )
 
-    here = 0.25 * off_ref[0 * R * C + row * C + col].astype(F32)
     below_row = jnp.minimum(row + 1, R - 1)
     right_col = jnp.minimum(col + 1, C - 1)
     stepx, stepy = [], []
     for c in range(CH):
-        here = 0.25 * off_ref[c * R * C + row * C + col].astype(F32)
-        stepx.append(0.25 * off_ref[c * R * C + below_row * C + col].astype(F32) - here)
-        stepy.append(0.25 * off_ref[c * R * C + row * C + right_col].astype(F32) - here)
+        here = 0.25 * off_ref[c, row, col].astype(F32)
+        stepx.append(0.25 * off_ref[c, below_row, col].astype(F32) - here)
+        stepy.append(0.25 * off_ref[c, row, right_col].astype(F32) - here)
     ER = 32
 
     def edge_rows(t, carry):
@@ -117,6 +125,8 @@
             E[CH + c, pl.ds(b0, ER), 0:TW] = ey
         return carry
 
+    for cp in loads:
+        cp.wait()
     lax.fori_loop(0, TH // ER, edge_rows, 0)
 
     lane = iota((half, LANES), 1)
@@ -240,10 +250,9 @@
     HR = 40
     nchunk = (TH + 16) // HR
 
-    XA[:, 0:8, :] = jnp.zeros((CH, 8, W), F32)
-    XA[:, PAD + TH + 8 :, :] = jnp.zeros((CH, 8, W), F32)
-    XB[:, 0:8, :] = jnp.zeros((CH, 8, W), F32)
-    XB[:, PAD + TH + 8 :, :] = jnp.zeros((CH, 8, W), F32)
+    for buf in (XA, XB):
+        buf[:, :, 0:8, :] = jnp.zeros((CH, Q, 8, LANES), F32)
+        buf[:, :, PAD + TH + 8 :, :] = jnp.zeros((CH, Q, 8, LANES), F32)
 
     def source_rows(t, carry):
         b0 = pl.multiple_of(8 + t * HR, 8)
@@ -254,22 +263,33 @@
             s = (wide[7 : 7 + HR] - wide[8:]) + (pltpu.roll(ey, 1, 1) - ey)
             s = s * d
             S[c, pl.ds(b0, HR), :] = s
-            XA[c, pl.ds(b0, HR), :] = s
+            for q in range(Q):
+                XA[c, q, pl.ds(b0, HR), :] = s[:, q * LANES : (q + 1) * LANES]
         return carry
 
     lax.fori_loop(0, nchunk, source_rows, 0)
+
+    def neighbours(src, c, b0, count, tiles):
+        at_rows = lambda by: pl.ds(b0 + by, count)
+        lanes = iota((count, LANES), 1)
+        mids = [src[c, q, at_rows(0), :] for q in range(Q)]
+        back = [pltpu.roll(m, 1, 1) for m in mids]
+        fore = [pltpu.roll(m, LANES - 1, 1) for m in mids]
+        sums = []
+        for q in range(tiles):
+            before = jnp.where(lanes == 0, back[(q - 1) % Q], back[q])
+            after = jnp.where(lanes == LANES - 1, fore[(q + 1) % Q], fore[q])
+            sums.append(src[c, q, at_rows(-1), :] + src[c, q, at_rows(1), :] + (before + after))
+        return sums
 
     def sweep(src, dst):
         def rows(t, carry):
             b0 = pl.multiple_of(8 + t * HR, 8)
             d = inv[pl.ds(b0, HR), :]
             for c in range(CH):
-                wide = src[c, pl.ds(pl.multiple_of(b0 - 8, 8), HR + 16), :]
-                mid = wide[8 : 8 + HR]
-                nb = (wide[7 : 7 + HR] + wide[9 : 9 + HR]) + (
-                    pltpu.roll(mid, 1, 1) + pltpu.roll(mid, W - 1, 1)
-                )
-                dst[c, pl.ds(b0, HR), :] = S[c, pl.ds(b0, HR), :] + nb * d
+                for q, nb in enumerate(neighbours(src, c, b0, HR, Q)):
+                    cut = slice(q * LANES, (q + 1) * LANES)
+                    dst[c, q, pl.ds(b0, HR), :] = S[c, pl.ds(b0, HR), cut] + nb * d[:, cut]
             return carry
 
         lax.fori_loop(0, nchunk, rows, 0)
@@ -329,11 +349,9 @@
         o0 = pl.multiple_of(t * LR, 8)
         d = inv[pl.ds(b0, LR), 0:TW]
         for c in range(CH):
-            wide = XA[c, pl.ds(pl.multiple_of(b0 - 8, 8), LR + 16), :]
-            mid = wide[8 : 8 + LR]
-            side = pltpu.roll(mid, 1, 1) + pltpu.roll(mid, W - 1, 1)
-            nb = (wide[7 : 7 + LR] + wide[9 : 9 + LR])[:, 0:TW] + side[:, 0:TW]
-            ts_ref[c, pl.ds(o0, LR), :] = S[c, pl.ds(b0, LR), 0:TW] + nb * d
+            for q, nb in enumerate(neighbours(XA, c, b0, LR, Q - 1)):
+                cut = slice(q * LANES, (q + 1) * LANES)
+                ts_ref[c, pl.ds(o0, LR), cut] = S[c, pl.ds(b0, LR), cut] + nb * d[:, cut]
         return carry
 
     lax.fori_loop(0, TH // LR, last_rows, 0)
@@ -356,66 +374,61 @@
 
 def last_kernel(
     dims,
-    pos_ref, sp_ref, ts_ref, tb_ref, mu_ref, cxk_ref, cxr_ref, cyb_ref, cys_ref, cyk_ref,
-    out_ref, H,
+    pos_ref, sp_ref, ts_ref, tb_ref, mu_ref, cxk_ref, cxr_ref, cyb_ref, cys_ref,
+    out_ref, H, ends, sides,
 ):
     R, C, CH, TH, TW, screen = dims
-    W = TW + LANES
+    W = TH + LANES
+    N = 16 * CH
     highest = lax.Precision.HIGHEST
+    channel = pl.program_id(0)
     row, col = pos_ref[0], pos_ref[1]
     top, bottom = row == 0, row == R - 1
     left, right = col == 0, col == C - 1
-    sp = sp_ref[...]
-    coeffs = sp * tb_ref[0]
-    moved = sp * tb_ref[1]
-
-    hi, lo = split(moved)
-    both = jnp.concatenate([hi, lo], axis=1)
-    h = jnp.dot(cxr_ref[...], jnp.concatenate([both, both], axis=0), preferred_element_type=F32)
-    H[...] = h[:, :M] + h[:, M:]
-
-    @pl.when(top | bottom)
+
+    def coeffs(c):
+        return sp_ref[c * M : (c + 1) * M, :] * tb_ref[0]
+
+    @pl.when((channel == 0) & (top | bottom))
     def _():
-        strip = jnp.where(top, 1, 0)
-        tab = cxk_ref[...]
-        lanes = jnp.where(top, 0.0, 1.0)
-        first, last = tab[:, 0:LANES], tab[:, TW - LANES : TW]
-        pick = jnp.where(top, first, last)
-        u = lax.dot_general(
-            pick, coeffs, (((0,), (0,)), ((), ())), precision=highest, preferred_element_type=F32
-        )
-        u = jnp.where(top, u[0:16], u[LANES - 16 :])
-        r = iota((16, M), 0)
+        pick = jnp.where(
+            top, cxr_ref[0:16, :].astype(F32), cxr_ref[TH - 16 : TH, :].astype(F32)
+        )
+        pick = pick[:, :M] + pick[:, M:]
+        u = jnp.concatenate(
+            [
+                jnp.dot(pick, coeffs(c), precision=highest, preferred_element_type=F32)
+                for c in range(CH)
+            ],
+            axis=0,
+        )
+        r = iota((N, M), 0) % 16
         edge = (top & (r == 0)) | (bottom & (r == 15))
         scale = 1.0 / (screen + jnp.where(edge, 3.0, 4.0))
         own = 2.0 - mu_ref[...]
         for _ in range(SWEEPS):
             up = jnp.where(r == 0, 0.0, pltpu.roll(u, 1, 0))
-            down = jnp.where(r == 15, 0.0, pltpu.roll(u, 15, 0))
+            down = jnp.where(r == 15, 0.0, pltpu.roll(u, N - 1, 0))
             u = (up + down + own * u) * scale
-
-        @pl.when(top)
-        def _():
-            H[0:8, :] = u[0:8]
-
-        @pl.when(bottom)
-        def _():
-            H[TH - 8 : TH, :] = u[8:16]
-
-    hh, hl = split(H[...])
-    lhs = jnp.concatenate([hh, hl, hh], axis=1)
-    out_ref[0] = jnp.dot(lhs, cyb_ref[...], preferred_element_type=F32) + ts_ref[0]
-
-    @pl.when(left | right)
+        ends[...] = u
+
+    @pl.when((channel == 0) & (left | right))
     def _():
         cy = jnp.where(left, cys_ref[0:16, :], cys_ref[TW - 16 : TW, :])
-        z = lax.dot_general(
-            cy, coeffs, (((1,), (1,)), ((), ())), precision=highest, preferred_element_type=F32
+        z = jnp.concatenate(
+            [
+                lax.dot_general(
+                    cy, coeffs(c), (((1,), (1,)), ((), ())),
+                    precision=highest, preferred_element_type=F32,
+                )
+                for c in range(CH)
+            ],
+            axis=0,
         )
         w = jnp.dot(z, cxk_ref[...], precision=highest, preferred_element_type=F32)
-        r = iota((16, W), 0)
-        lanes = iota((16, W), 1)
-        place = jnp.where(lanes < TW + 8, lanes, lanes - W) + row * TH
+        r = iota((N, W), 0) % 16
+        lanes = iota((N, W), 1)
+        place = jnp.where(lanes < TH + 8, lanes, lanes - W) + row * TH
         inside = (place >= 0) & (place < R * TH)
         cx = (place > 0).astype(F32) + (place < R * TH - 1).astype(F32)
         edge = (left & (r == 0)) | (right & (r == 15))
@@ -423,26 +436,43 @@
         w = jnp.where(inside, w, 0.0)
         for _ in range(SWEEPS):
             up = jnp.where(r == 0, 0.0, pltpu.roll(w, 1, 0))
-            down = jnp.where(r == 15, 0.0, pltpu.roll(w, 15, 0))
+            down = jnp.where(r == 15, 0.0, pltpu.roll(w, N - 1, 0))
             w = (up + down + (pltpu.roll(w, 1, 1) + pltpu.roll(w, W - 1, 1))) * scale
-        wide = jnp.concatenate(
-            [w[:, 0:TW], jnp.zeros((LANES - 16, TW), F32)], axis=0
-        )
-        wt = wide.T
-        lane = iota((TW, LANES), 1)
-
-        @pl.when(left)
-        def _():
-            ts = ts_ref[0, :, 0:LANES]
-            out_ref[0, :, 0:LANES] = jnp.where(lane < 8, wt + ts, out_ref[0, :, 0:LANES])
-
-        @pl.when(right)
-        def _():
-            ts = ts_ref[0, :, TW - LANES : TW]
-            turned = pltpu.roll(wt, LANES - 16, 1)
-            out_ref[0, :, TW - LANES : TW] = jnp.where(
-                lane >= LANES - 8, turned + ts, out_ref[0, :, TW - LANES : TW]
-            )
+        wide = jnp.concatenate([w[:, 0:TH], jnp.zeros((LANES - N, TH), F32)], axis=0)
+        sides[...] = wide.T
+
+    moved = sp_ref[pl.ds(pl.multiple_of(channel * M, M), M), :] * tb_ref[1]
+    hi, lo = split(moved)
+    both = jnp.concatenate([hi, lo], axis=1)
+    h = jnp.dot(cxr_ref[...], jnp.concatenate([both, both], axis=0), preferred_element_type=F32)
+    H[...] = h[:, :M] + h[:, M:]
+
+    @pl.when(top)
+    def _():
+        H[0:8, :] = ends[pl.ds(pl.multiple_of(channel * 16, 8), 8), :]
+
+    @pl.when(bottom)
+    def _():
+        H[TH - 8 : TH, :] = ends[pl.ds(pl.multiple_of(channel * 16 + 8, 8), 8), :]
+
+    hh, hl = split(H[...])
+    lhs = jnp.concatenate([hh, hl, hh], axis=1)
+    out_ref[0] = jnp.dot(lhs, cyb_ref[...], preferred_element_type=F32) + ts_ref[0]
+    lane = iota((TH, LANES), 1)
+
+    @pl.when(left)
+    def _():
+        turned = pltpu.roll(sides[...], lax.rem(LANES - 16 * channel, LANES), 1)
+        ts = ts_ref[0, :, 0:LANES]
+        out_ref[0, :, 0:LANES] = jnp.where(lane < 8, turned + ts, out_ref[0, :, 0:LANES])
+
+    @pl.when(right)
+    def _():
+        turned = pltpu.roll(sides[...], LANES - 16 - 16 * channel, 1)
+        ts = ts_ref[0, :, TW - LANES : TW]
+        out_ref[0, :, TW - LANES : TW] = jnp.where(
+            lane >= LANES - 8, turned + ts, out_ref[0, :, TW - LANES : TW]
+        )
 
 
 def body(grad_x, grad_y, seam_mask, tile_offset, tables):
@@ -457,7 +487,7 @@
     crows = modes // C
     nparts = min(R, crows // 8)
     prow = crows // nparts
-    ty, tx, tb, mu, cxk, cxr, cyb, cys, cyk = tables
+    ty, tx, tb, mu, cxk, cxr, cyb, cys = tables
     vmem = pl.BlockSpec(memory_space=pltpu.VMEM)
     smem = pl.BlockSpec(memory_space=pltpu.SMEM)
     anys = pl.BlockSpec(memory_space=pl.ANY)
@@ -469,13 +499,16 @@
             jax.ShapeDtypeStruct((CH, TH, TW), F32),
             jax.ShapeDtypeStruct((modes, M), F32),
         ),
-        in_specs=[vmem, vmem, vmem, smem, anys, anys],
+        in_specs=[anys, anys, anys, smem, anys, anys],
         out_specs=(vmem, vmem),
         scratch_shapes=[
+            pltpu.VMEM((CH, TH, TW), BF16),
+            pltpu.VMEM((CH, TH, TW), BF16),
+            pltpu.VMEM((TH, TW), jnp.int32),
             pltpu.VMEM((2 * CH, rows, W), F32),
             pltpu.VMEM((CH, rows, W), F32),
-            pltpu.VMEM((CH, rows, W), F32),
-            pltpu.VMEM((CH, rows, W), F32),
+            pltpu.VMEM((CH, W // LANES, rows, LANES), F32),
+            pltpu.VMEM((CH, W // LANES, rows, LANES), F32),
             pltpu.VMEM((rows, W), F32),
             pltpu.VMEM((TW, 4 * M), BF16),
             pltpu.VMEM((2 * M, 2 * TH), BF16),
@@ -487,42 +520,44 @@
             pltpu.VMEM((R, prow, M), F32),
             pltpu.VMEM((prow, M), F32),
             pltpu.VMEM((crows, M), F32),
-            dma((2,)), dma((2,)), dma((2,)), dma((2,)), dma((2,)),
+            dma((3,)), dma((2,)), dma((2,)), dma((2,)), dma((2,)), dma((2,)),
             dma((C,)), dma((C,)), dma((R,)), dma((R,)),
             dma((R,)), dma((R,)), dma((C,)), dma((C,)),
         ],
         compiler_params=pltpu.CompilerParams(
-            collective_id=0, has_side_effects=True, vmem_limit_bytes=48 * 2**20
+            collective_id=0, has_side_effects=True, vmem_limit_bytes=58 * 2**20
         ),
         name="sums_and_sweeps",
-    )(grad_x, grad_y, seam_mask, tile_offset.reshape(-1), ty, tx)
+    )(grad_x, grad_y, seam_mask, tile_offset, ty, tx)
 
     pos = jnp.stack([lax.axis_index("row"), lax.axis_index("col")]).astype(jnp.int32)
-    here = lambda i, p: (p[0], 0)
     spec = pltpu.PrefetchScalarGridSpec(
         num_scalar_prefetch=1,
         grid=(CH,),
         in_specs=[
-            pl.BlockSpec((M, M), lambda i, p: (i, 0)),
+            pl.BlockSpec((modes, M), lambda i, p: (0, 0)),
             pl.BlockSpec((1, TH, TW), lambda i, p: (i, 0, 0)),
             pl.BlockSpec((2, M, M), lambda i, p: (0, 0, 0)),
             pl.BlockSpec((1, M), lambda i, p: (0, 0)),
-            pl.BlockSpec((M, W), lambda i, p: (p[0], 0)),
+            pl.BlockSpec((M, TH + LANES), lambda i, p: (p[0], 0)),
             pl.BlockSpec((TH, 2 * M), lambda i, p: (p[0], 0)),
             pl.BlockSpec((3 * M, TW), lambda i, p: (0, p[1])),
             pl.BlockSpec((TW, M), lambda i, p: (p[1], 0)),
-            pl.BlockSpec((8, LANES), lambda i, p: (0, 0)),
         ],
         out_specs=pl.BlockSpec((1, TH, TW), lambda i, p: (i, 0, 0)),
-        scratch_shapes=[pltpu.VMEM((TH, M), F32)],
+        scratch_shapes=[
+            pltpu.VMEM((TH, M), F32),
+            pltpu.VMEM((16 * CH, M), F32),
+            pltpu.VMEM((TH, LANES), F32),
+        ],
     )
     return pl.pallas_call(
         functools.partial(last_kernel, dims),
         grid_spec=spec,
         out_shape=jax.ShapeDtypeStruct((CH, TH, TW), F32),
-        compiler_params=pltpu.CompilerParams(vmem_limit_bytes=40 * 2**20),
+        compiler_params=pltpu.CompilerParams(vmem_limit_bytes=58 * 2**20),
         name="synthesis",
-    )(pos, sp, ts, tb, mu, cxk, cxr, cyb, cys, cyk)
+    )(pos, sp, ts, tb, mu, cxk, cxr, cyb, cys)
 
 
 def solution(mesh):
@@ -569,7 +604,6 @@
             jnp.asarray(cxk.reshape(R * M, W).astype(np.float32)),
             jnp.asarray(cxr), jnp.asarray(cyb),
             jnp.asarray(cy.astype(np.float32)),
-            jnp.zeros((8, LANES), F32),
         )
         f = jax.shard_map(body, mesh=mesh, in_specs=in_specs, out_specs=out_specs, check_vma=False)
         return f(grad_x, grad_y, seam_mask, tile_offset, tables)

time: 47.1 us -> 38.4 us (0.82)
  local copies, waits for them, and re-layouts: 8.49 us -> 0 us
  Pallas kernels: 38.1 us -> 37.5 us
  other arithmetic: 0.07 us -> 0.65 us
    unnamed x24 -> x0, local copies, waits for them, and re-layouts: 7.71 us -> none
    reshape x1 -> x0, local copies, waits for them, and re-layouts: 0.78 us -> none  [body(): tile_offset.reshape(-1)]
    another operation x1, other arithmetic: 0.07 us -> 0.65 us  [body(): jnp.stack([lax.axis_index('row'), lax.axis_index('col')]).astype(jnp.int32)]
where the time goes in v2:
time: 38.4 us; the launch traced here: 38.1 us
  Pallas kernels  37.5 us (98%)
  other arithmetic  0.65 us (2%)
    pallas_call x1, Pallas kernels, body(): pl.pallas_call(functools.partial(first_kernel, dims), out_shape=(jax.Shap...  29.7 us
    pallas_call x1, Pallas kernels, body(): pl.pallas_call(functools.partial(last_kernel, dims), grid_spec=spec, out_...  7.78 us

profile of v2, /device:TPU:0, one launch (start us, length us, event | category | flops | bytes accessed | tf_op | source)
XLA Modules:
  0.0 38.1 jit_solution(16239635147331337404)
XLA Ops:
  0.0 0.6 %pad_add_fusion.pos_ref = s32[2]{0:T(128)} fusion(s32[1]{0:T(128)} %bitcast.1, s32[1]{0:T(128)} %bitcast), kind=kLoop, calls=%fused_computation | loop fusion | flops 2 | bytes 16 | tf_op jit(solution)/shard_map/stack | solution.py:533
  0.6 29.7 %sums_and_sweeps.1 = (f32[3,384,384]{2,1,0:T(8,128)}, f32[384,128]{1,0:T(8,128)}) custom-call(bf16[3,384,384]{2,1,0:T(8,128)(2,1)} %gx_hbm.1, bf16[3,384,384]{2,1,0:T(8,128)(2,1)} %gy_hbm.1, s32[384,384]{1,0:T(8,128)} %mask_hbm.1, s32[3,4,4]{2,1,0:T(4,128)} %off_ref.1, bf16[1536,512]{1,0:T(8,128)(2,1)} %constant.23.clone.ty_hbm, ...), custom_call_target="tpu_custom_call" | custom-call | tf_op jit(solution)/shard_map/sums_and_sweeps/pallas_call | solution.py:496
  30.3 7.8 %synthesis.1 = f32[3,384,384]{2,1,0:T(8,128)} custom-call(s32[2]{0:T(128)} %pad_add_fusion.pos_ref, f32[384,128]{1,0:T(8,128)} %get-tuple-element.7.sp_ref, f32[3,384,384]{2,1,0:T(8,128)} %get-tuple-element.8.ts_ref, f32[2,128,128]{2,1,0:T(8,128)} %constant.25.clone.tb_ref, f32[1,128]{1,0:T(1,128)} %constant.26.clone.mu_ref, ...), custom_call_target="tpu_custom_call" | custom-call | tf_op jit(solution)/shard_map/synthesis/pallas_call | solution.py:554

commit v3 on v2

--- a/solution.py
+++ b/solution.py
@@ -106,7 +106,7 @@
         here = 0.25 * off_ref[c, row, col].astype(F32)
         stepx.append(0.25 * off_ref[c, below_row, col].astype(F32) - here)
         stepy.append(0.25 * off_ref[c, row, right_col].astype(F32) - here)
-    ER = 32
+    ER = 96
 
     def edge_rows(t, carry):
         r0 = pl.multiple_of(t * ER, ER)
@@ -156,7 +156,28 @@
     pl.when(col < C - 1)(to_right.start)
     pl.when(col > 0)(to_left.start)
 
-    IR = 32
+    def row_copies(lanes, first):
+        below = pltpu.make_async_remote_copy(
+            src_ref=E.at[:, pl.ds(PAD + TH - 8, 8), lanes],
+            dst_ref=E.at[:, pl.ds(PAD - 8, 8), lanes],
+            send_sem=rs_send.at[first], recv_sem=rs_recv.at[first],
+            device_id=at(jnp.minimum(row + 1, R - 1), col), device_id_type=MESH,
+        )
+        above = pltpu.make_async_remote_copy(
+            src_ref=E.at[:, pl.ds(PAD, 8), lanes],
+            dst_ref=E.at[:, pl.ds(PAD + TH, 8), lanes],
+            send_sem=rs_send.at[first + 1], recv_sem=rs_recv.at[first + 1],
+            device_id=at(jnp.maximum(row - 1, 0), col), device_id_type=MESH,
+        )
+        return below, above
+
+    row_main = row_copies(pl.ds(0, TW), 0)
+    row_corner = row_copies(pl.ds(TW, LANES), 2)
+
+    pl.when(row < R - 1)(row_main[0].start)
+    pl.when(row > 0)(row_main[1].start)
+
+    IR = 104
     def inv_rows(t, carry):
         r0 = pl.multiple_of(t * IR, IR)
         places = iota((IR, 1), 0) + r0 - PAD + row * TH
@@ -174,7 +195,7 @@
 
     ty_copy.wait()
     tx_copy.wait()
-    for c in range(CH):
+    def forward(c):
         hs = []
         for d in range(2):
             e = E[d * CH + c, PAD : PAD + TH, 0:TW].astype(BF16)
@@ -185,16 +206,7 @@
         o = jnp.dot(tx[...], jnp.concatenate([hi, lo], axis=1), preferred_element_type=F32)
         part[c * M : (c + 1) * M, :] = (o[:M, :M] + o[M:, :M]) + (o[:M, M:] + o[M:, M:])
 
-    p1 = []
-    for off in range(1, C):
-        d = lax.rem(col + off, C)
-        cp = pltpu.make_async_remote_copy(
-            src_ref=part.at[pl.ds(pl.multiple_of(d * crows, 8), crows)], dst_ref=r1.at[off],
-            send_sem=p1s.at[off], recv_sem=p1r.at[off],
-            device_id=at(row, d), device_id_type=MESH,
-        )
-        cp.start()
-        p1.append(cp)
+    forward(0)
 
     pl.when(col > 0)(to_right.wait_recv)
     pl.when(col < C - 1)(to_left.wait_recv)
@@ -207,18 +219,22 @@
             if spot:
                 right = pltpu.roll(right, LANES - spot, 1)
             E[a, rows, TW:W] = jnp.where(lane < 8, right, jnp.where(lane >= 120, left, 0.0))
-    to_below = pltpu.make_async_remote_copy(
-        src_ref=E.at[:, pl.ds(PAD + TH - 8, 8), :], dst_ref=E.at[:, pl.ds(PAD - 8, 8), :],
-        send_sem=rs_send.at[0], recv_sem=rs_recv.at[0],
-        device_id=at(jnp.minimum(row + 1, R - 1), col), device_id_type=MESH,
-    )
-    to_above = pltpu.make_async_remote_copy(
-        src_ref=E.at[:, pl.ds(PAD, 8), :], dst_ref=E.at[:, pl.ds(PAD + TH, 8), :],
-        send_sem=rs_send.at[1], recv_sem=rs_recv.at[1],
-        device_id=at(jnp.maximum(row - 1, 0), col), device_id_type=MESH,
-    )
-    pl.when(row < R - 1)(to_below.start)
-    pl.when(row > 0)(to_above.start)
+    pl.when(row < R - 1)(row_corner[0].start)
+    pl.when(row > 0)(row_corner[1].start)
+
+    for c in range(1, CH):
+        forward(c)
+
+    p1 = []
+    for off in range(1, C):
+        d = lax.rem(col + off, C)
+        cp = pltpu.make_async_remote_copy(
+            src_ref=part.at[pl.ds(pl.multiple_of(d * crows, 8), crows)], dst_ref=r1.at[off],
+            send_sem=p1s.at[off], recv_sem=p1r.at[off],
+            device_id=at(row, d), device_id_type=MESH,
+        )
+        cp.start()
+        p1.append(cp)
 
     for cp in p1:
         cp.wait_recv()
@@ -245,9 +261,9 @@
         guarded(d < nparts, cp.start)
         p2.append((cp, d))
 
-    pl.when(row > 0)(to_below.wait_recv)
-    pl.when(row < R - 1)(to_above.wait_recv)
+    SR = 40
     HR = 40
+    schunk = (TH + 16) // SR
     nchunk = (TH + 16) // HR
 
     for buf in (XA, XB):
@@ -255,19 +271,24 @@
         buf[:, :, PAD + TH + 8 :, :] = jnp.zeros((CH, Q, 8, LANES), F32)
 
     def source_rows(t, carry):
-        b0 = pl.multiple_of(8 + t * HR, 8)
-        d = inv[pl.ds(b0, HR), :]
+        b0 = pl.multiple_of(8 + t * SR, 8)
+        d = inv[pl.ds(b0, SR), :]
         for c in range(CH):
-            wide = E[c, pl.ds(pl.multiple_of(b0 - 8, 8), HR + 8), :]
-            ey = E[CH + c, pl.ds(b0, HR), :]
-            s = (wide[7 : 7 + HR] - wide[8:]) + (pltpu.roll(ey, 1, 1) - ey)
+            wide = E[c, pl.ds(pl.multiple_of(b0 - 8, 8), SR + 8), :]
+            ey = E[CH + c, pl.ds(b0, SR), :]
+            s = (wide[7 : 7 + SR] - wide[8:]) + (pltpu.roll(ey, 1, 1) - ey)
             s = s * d
-            S[c, pl.ds(b0, HR), :] = s
+            S[c, pl.ds(b0, SR), :] = s
             for q in range(Q):
-                XA[c, q, pl.ds(b0, HR), :] = s[:, q * LANES : (q + 1) * LANES]
+                XA[c, q, pl.ds(b0, SR), :] = s[:, q * LANES : (q + 1) * LANES]
         return carry
 
-    lax.fori_loop(0, nchunk, source_rows, 0)
+    lax.fori_loop(1, schunk - 1, source_rows, 0)
+    for below, above in (row_main, row_corner):
+        pl.when(row > 0)(below.wait_recv)
+        pl.when(row < R - 1)(above.wait_recv)
+    source_rows(0, 0)
+    source_rows(schunk - 1, 0)
 
     def neighbours(src, c, b0, count, tiles):
         at_rows = lambda by: pl.ds(b0 + by, count)
@@ -283,16 +304,16 @@
         return sums
 
     def sweep(src, dst):
-        def rows(t, carry):
-            b0 = pl.multiple_of(8 + t * HR, 8)
-            d = inv[pl.ds(b0, HR), :]
-            for c in range(CH):
+        def one(c, carry):
+            for t in range(nchunk):
+                b0 = 8 + t * HR
+                d = inv[b0 : b0 + HR, :]
                 for q, nb in enumerate(neighbours(src, c, b0, HR, Q)):
                     cut = slice(q * LANES, (q + 1) * LANES)
-                    dst[c, q, pl.ds(b0, HR), :] = S[c, pl.ds(b0, HR), cut] + nb * d[:, cut]
+                    dst[c, q, b0 : b0 + HR, :] = S[c, b0 : b0 + HR, cut] + nb * d[:, cut]
             return carry
 
-        lax.fori_loop(0, nchunk, rows, 0)
+        lax.fori_loop(0, CH, one, 0)
 
     sweep(XA, XB)
     sweep(XB, XA)
@@ -342,26 +363,28 @@
 
     sweep(XA, XB)
     sweep(XB, XA)
-    LR = 32
-
-    def last_rows(t, carry):
-        b0 = pl.multiple_of(PAD + t * LR, 8)
-        o0 = pl.multiple_of(t * LR, 8)
-        d = inv[pl.ds(b0, LR), 0:TW]
-        for c in range(CH):
+    LR = 48
+
+    def last(c, carry):
+        for t in range(TH // LR):
+            b0 = PAD + t * LR
+            d = inv[b0 : b0 + LR, 0:TW]
             for q, nb in enumerate(neighbours(XA, c, b0, LR, Q - 1)):
                 cut = slice(q * LANES, (q + 1) * LANES)
-                ts_ref[c, pl.ds(o0, LR), cut] = S[c, pl.ds(b0, LR), cut] + nb * d[:, cut]
+                ts_ref[c, t * LR : (t + 1) * LR, cut] = (
+                    S[c, b0 : b0 + LR, cut] + nb * d[:, cut]
+                )
         return carry
 
-    lax.fori_loop(0, TH // LR, last_rows, 0)
+    lax.fori_loop(0, CH, last, 0)
 
     for cp in p4:
         cp.wait_recv()
     pl.when(col < C - 1)(to_right.wait_send)
     pl.when(col > 0)(to_left.wait_send)
-    pl.when(row < R - 1)(to_below.wait_send)
-    pl.when(row > 0)(to_above.wait_send)
+    for below, above in (row_main, row_corner):
+        pl.when(row < R - 1)(below.wait_send)
+        pl.when(row > 0)(above.wait_send)
     for cp in p1:
         cp.wait_send()
     for cp, d in p2:
@@ -520,7 +543,7 @@
             pltpu.VMEM((R, prow, M), F32),
             pltpu.VMEM((prow, M), F32),
             pltpu.VMEM((crows, M), F32),
-            dma((3,)), dma((2,)), dma((2,)), dma((2,)), dma((2,)), dma((2,)),
+            dma((3,)), dma((2,)), dma((2,)), dma((2,)), dma((4,)), dma((4,)),
             dma((C,)), dma((C,)), dma((R,)), dma((R,)),
             dma((R,)), dma((R,)), dma((C,)), dma((C,)),
         ],

time: 38.4 us -> 37.3 us (0.971)
  Pallas kernels: 37.5 us -> 36.4 us
    pallas_call x1, Pallas kernels: 29.7 us -> 28.6 us  [body(): pl.pallas_call(functools.partial(first_kernel, dims), out_shape=(jax.Shap...]
where the time goes in v3:
time: 37.3 us; the launch traced here: 37 us
  Pallas kernels  36.4 us (98%)
  other arithmetic  0.65 us (2%)
    pallas_call x1, Pallas kernels, body(): pl.pallas_call(functools.partial(first_kernel, dims), out_shape=(jax.Shap...  28.6 us
    pallas_call x1, Pallas kernels, body(): pl.pallas_call(functools.partial(last_kernel, dims), grid_spec=spec, out_...  7.78 us

profile of v3, /device:TPU:0, one launch (start us, length us, event | category | flops | bytes accessed | tf_op | source)
XLA Modules:
  0.0 37.0 jit_solution(18143326302095131042)
XLA Ops:
  0.0 0.6 %pad_add_fusion.pos_ref = s32[2]{0:T(128)} fusion(s32[1]{0:T(128)} %bitcast.1, s32[1]{0:T(128)} %bitcast), kind=kLoop, calls=%fused_computation | loop fusion | flops 2 | bytes 16 | tf_op jit(solution)/shard_map/stack | solution.py:556
  0.6 28.6 %sums_and_sweeps.1 = (f32[3,384,384]{2,1,0:T(8,128)}, f32[384,128]{1,0:T(8,128)}) custom-call(bf16[3,384,384]{2,1,0:T(8,128)(2,1)} %gx_hbm.1, bf16[3,384,384]{2,1,0:T(8,128)(2,1)} %gy_hbm.1, s32[384,384]{1,0:T(8,128)} %mask_hbm.1, s32[3,4,4]{2,1,0:T(4,128)} %off_ref.1, bf16[1536,512]{1,0:T(8,128)(2,1)} %constant.23.clone.ty_hbm, ...), custom_call_target="tpu_custom_call" | custom-call | tf_op jit(solution)/shard_map/sums_and_sweeps/pallas_call | solution.py:519
  29.3 7.8 %synthesis.1 = f32[3,384,384]{2,1,0:T(8,128)} custom-call(s32[2]{0:T(128)} %pad_add_fusion.pos_ref, f32[384,128]{1,0:T(8,128)} %get-tuple-element.7.sp_ref, f32[3,384,384]{2,1,0:T(8,128)} %get-tuple-element.8.ts_ref, f32[2,128,128]{2,1,0:T(8,128)} %constant.25.clone.tb_ref, f32[1,128]{1,0:T(1,128)} %constant.26.clone.mu_ref, ...), custom_call_target="tpu_custom_call" | custom-call | tf_op jit(solution)/shard_map/synthesis/pallas_call | solution.py:577

commit v4 on v3

--- a/solution.py
+++ b/solution.py
@@ -177,6 +177,33 @@
     pl.when(row < R - 1)(row_main[0].start)
     pl.when(row > 0)(row_main[1].start)
 
+    ty_copy.wait()
+    tx_copy.wait()
+    def forward(c):
+        hs = []
+        for d in range(2):
+            e = E[d * CH + c, PAD : PAD + TH, 0:TW].astype(BF16)
+            h = jnp.dot(e, ty[:, d * 2 * M : (d + 1) * 2 * M], preferred_element_type=F32)
+            hs.append(h[:, :M] + h[:, M:])
+        h = jnp.concatenate(hs, axis=0)
+        hi, lo = split(h)
+        o = jnp.dot(tx[...], jnp.concatenate([hi, lo], axis=1), preferred_element_type=F32)
+        part[c * M : (c + 1) * M, :] = (o[:M, :M] + o[M:, :M]) + (o[:M, M:] + o[M:, M:])
+
+    for c in range(CH):
+        forward(c)
+
+    p1 = []
+    for off in range(1, C):
+        d = lax.rem(col + off, C)
+        cp = pltpu.make_async_remote_copy(
+            src_ref=part.at[pl.ds(pl.multiple_of(d * crows, 8), crows)], dst_ref=r1.at[off],
+            send_sem=p1s.at[off], recv_sem=p1r.at[off],
+            device_id=at(row, d), device_id_type=MESH,
+        )
+        cp.start()
+        p1.append(cp)
+
     IR = 104
     def inv_rows(t, carry):
         r0 = pl.multiple_of(t * IR, IR)
@@ -193,21 +220,6 @@
 
     lax.fori_loop(0, (TH + 2 * PAD) // IR, inv_rows, 0)
 
-    ty_copy.wait()
-    tx_copy.wait()
-    def forward(c):
-        hs = []
-        for d in range(2):
-            e = E[d * CH + c, PAD : PAD + TH, 0:TW].astype(BF16)
-            h = jnp.dot(e, ty[:, d * 2 * M : (d + 1) * 2 * M], preferred_element_type=F32)
-            hs.append(h[:, :M] + h[:, M:])
-        h = jnp.concatenate(hs, axis=0)
-        hi, lo = split(h)
-        o = jnp.dot(tx[...], jnp.concatenate([hi, lo], axis=1), preferred_element_type=F32)
-        part[c * M : (c + 1) * M, :] = (o[:M, :M] + o[M:, :M]) + (o[:M, M:] + o[M:, M:])
-
-    forward(0)
-
     pl.when(col > 0)(to_right.wait_recv)
     pl.when(col < C - 1)(to_left.wait_recv)
     for a in range(2 * CH):
@@ -221,20 +233,6 @@
             E[a, rows, TW:W] = jnp.where(lane < 8, right, jnp.where(lane >= 120, left, 0.0))
     pl.when(row < R - 1)(row_corner[0].start)
     pl.when(row > 0)(row_corner[1].start)
-
-    for c in range(1, CH):
-        forward(c)
-
-    p1 = []
-    for off in range(1, C):
-        d = lax.rem(col + off, C)
-        cp = pltpu.make_async_remote_copy(
-            src_ref=part.at[pl.ds(pl.multiple_of(d * crows, 8), crows)], dst_ref=r1.at[off],
-            send_sem=p1s.at[off], recv_sem=p1r.at[off],
-            device_id=at(row, d), device_id_type=MESH,
-        )
-        cp.start()
-        p1.append(cp)
 
     for cp in p1:
         cp.wait_recv()

time: 37.3 us -> 35.4 us (0.949)
  Pallas kernels: 36.4 us -> 34.5 us
    pallas_call x1, Pallas kernels: 28.6 us -> 26.7 us  [body(): pl.pallas_call(functools.partial(first_kernel, dims), out_shape=(jax.Shap...]
where the time goes in v4:
time: 35.4 us; the launch traced here: 35.2 us
  Pallas kernels  34.5 us (97%)
  other arithmetic  0.65 us (2%)
    pallas_call x1, Pallas kernels, body(): pl.pallas_call(functools.partial(first_kernel, dims), out_shape=(jax.Shap...  26.7 us
    pallas_call x1, Pallas kernels, body(): pl.pallas_call(functools.partial(last_kernel, dims), grid_spec=spec, out_...  7.78 us

profile of v4, /device:TPU:0, one launch (start us, length us, event | category | flops | bytes accessed | tf_op | source)
XLA Modules:
  0.0 35.2 jit_solution(8497472379662100572)
XLA Ops:
  0.0 0.6 %pad_add_fusion.pos_ref = s32[2]{0:T(128)} fusion(s32[1]{0:T(128)} %bitcast.1, s32[1]{0:T(128)} %bitcast), kind=kLoop, calls=%fused_computation | loop fusion | flops 2 | bytes 16 | tf_op jit(solution)/shard_map/stack | solution.py:554
  0.6 26.7 %sums_and_sweeps.1 = (f32[3,384,384]{2,1,0:T(8,128)}, f32[384,128]{1,0:T(8,128)}) custom-call(bf16[3,384,384]{2,1,0:T(8,128)(2,1)} %gx_hbm.1, bf16[3,384,384]{2,1,0:T(8,128)(2,1)} %gy_hbm.1, s32[384,384]{1,0:T(8,128)} %mask_hbm.1, s32[3,4,4]{2,1,0:T(4,128)} %off_ref.1, bf16[1536,512]{1,0:T(8,128)(2,1)} %constant.23.clone.ty_hbm, ...), custom_call_target="tpu_custom_call" | custom-call | tf_op jit(solution)/shard_map/sums_and_sweeps/pallas_call | solution.py:517
  27.4 7.8 %synthesis.1 = f32[3,384,384]{2,1,0:T(8,128)} custom-call(s32[2]{0:T(128)} %pad_add_fusion.pos_ref, f32[384,128]{1,0:T(8,128)} %get-tuple-element.7.sp_ref, f32[3,384,384]{2,1,0:T(8,128)} %get-tuple-element.8.ts_ref, f32[2,128,128]{2,1,0:T(8,128)} %constant.25.clone.tb_ref, f32[1,128]{1,0:T(1,128)} %constant.26.clone.mu_ref, ...), custom_call_target="tpu_custom_call" | custom-call | tf_op jit(solution)/shard_map/synthesis/pallas_call | solution.py:575
